TPU v7x, 512 devices: a whole 4x4x16 slice. The times are simulated.
512 devices in a mesh: dp: 32 (over z, core), ctx: 16 (over x, y).
Axes of the slice: x: 4, y: 4, z: 16, core: 2. Of those that a mesh axis runs over, the one named last changes fastest.
Arguments:
- tokens: bfloat16 [65536, 4096], P(('dp', 'ctx')), parts along dimension 0, may hold values from -6 to 6
- selected: int32 [8192], P('dp'), parts along dimension 0, may hold values from 0 to 2047, as said below
- norm_gain: bfloat16 [4096], replicated, may hold values from 0.25 to 1.75
- router: bfloat16 [4096], replicated, may hold values from -0.09375 to 0.09375
- w_query: bfloat16 [4096, 2048], P(None, 'ctx'), as said below
- w_key: bfloat16 [4096, 512], P(None, 'ctx'), as said below
- w_value: bfloat16 [4096, 512], P(None, 'ctx'), may hold values from -0.09375 to 0.09375
- w_out: bfloat16 [2048, 4096], P('ctx'), may hold values from -0.125 to 0.125
Outputs:
- layer_out: bfloat16 [65536, 4096], P(('dp', 'ctx')), parts along dimension 0
There are 32 independent parts, one for each index of `dp`. A program takes and returns all parts, laid end to end along the dimension named above; an argument that names none is the same for every part. Nothing has to cross between parts.
Inputs may be any that keep to these rules, and one draw needn't show every extreme that they name: `selected`: strictly increasing; of each index's block of 128 positions at most 32 are listed, and one block has exactly 32. `w_query`: entries lie within six times 4096 to the power -0.5 of zero. `w_key`: entries lie within six times 4096 to the power -0.5 of zero.
All inputs are finite; a program needn't handle non-finite values.
Results may differ from a plain program's by a relative error of at most 0.0036.
Values may be sent and summed in bfloat16 or wider, within the bound.
No kernel may reach another device: no remote copies, remote signals or barrier semaphores. Data moves between devices by JAX's collectives and lax.ppermute only.
A program may use at most 64 MiB of HBM per device.

v0:
```python
import jax
import jax.numpy as jnp
from jax import lax
from jax.sharding import PartitionSpec as P

HS = 128
HQ = 16
KVH = 4
CAP = 32


def rotary(values, positions):
    width = values.shape[1]
    column = jnp.arange(width)
    pair = (column % HS // 2).astype(jnp.float32)
    inverse = jnp.exp(-(2.0 * pair / HS) * jnp.log(10000.0))
    angle = positions.astype(jnp.float32)[:, None] * inverse[None, :]
    cosine = jnp.cos(angle).reshape(values.shape[0], width // 2, 2)[:, :, 0]
    sine = jnp.sin(angle).reshape(values.shape[0], width // 2, 2)[:, :, 0]
    paired = values.reshape(values.shape[0], width // 2, 2)
    first = paired[:, :, 0]
    second = paired[:, :, 1]
    turned = jnp.stack([first * cosine - second * sine, first * sine + second * cosine], axis=2)
    return turned.reshape(values.shape[0], width)


def headwise(matrix):
    count = matrix.shape[0]
    return matrix.reshape(count, HS, KVH).transpose(0, 2, 1).reshape(count, KVH * HS)


def on_device(tokens, selected, norm_gain, router, w_query, w_key, w_value, w_out):
    devices = lax.axis_size("ctx")
    myself = lax.axis_index("ctx")
    tok_dev = tokens.shape[0]
    width = tokens.shape[1]
    total_sel = selected.shape[0]
    per_dev = total_sel // devices
    owner = selected // tok_dev
    my_owner = jnp.take(owner.reshape(per_dev, devices), myself, axis=1)
    starts = jnp.arange(devices, dtype=jnp.int32) * tok_dev
    first_of = jnp.sum((selected[None, :] < starts[:, None]).astype(jnp.int32), axis=1)
    my_first = jnp.take(first_of, myself)
    my_count = jnp.sum((owner == myself).astype(jnp.int32))
    padded_pos = jnp.concatenate([selected, jnp.zeros((CAP,), jnp.int32)])
    window = lax.dynamic_slice_in_dim(padded_pos, my_first, CAP)
    slot_live = jnp.arange(CAP) < my_count
    local_rows = jnp.where(slot_live, window - myself * tok_dev, 0)
    packed = jnp.where(slot_live[:, None], tokens[local_rows], jnp.zeros((), tokens.dtype))
    gathered = lax.all_gather(packed, "ctx", axis=0, tiled=True)
    source = owner * CAP + jnp.arange(total_sel, dtype=jnp.int32) - first_of[owner]
    routed = gathered[source]
    wide = routed.astype(jnp.float32)
    scale = lax.rsqrt(jnp.mean(wide * wide, axis=1, keepdims=True) + 1e-05)
    normed = (wide * scale * norm_gain.astype(jnp.float32)[None, :]).astype(jnp.bfloat16)
    query = rotary(jnp.dot(normed, w_query, preferred_element_type=jnp.float32), selected).astype(
        jnp.bfloat16
    )
    key_part = jnp.dot(normed, w_key, preferred_element_type=jnp.float32)
    value_part = jnp.dot(normed, w_value, preferred_element_type=jnp.float32)
    key_all, value_all = (
        lax.all_gather(key_part, "ctx", axis=1, tiled=True),
        lax.all_gather(value_part, "ctx", axis=1, tiled=True),
    )
    keys = rotary(headwise(key_all), selected).astype(jnp.bfloat16)
    values = headwise(value_all).astype(jnp.bfloat16)
    heads_here = query.shape[1] // HS
    groups = (myself * heads_here + jnp.arange(heads_here)) // (HQ // KVH)
    query_h = query.reshape(total_sel, heads_here, HS)
    keys_h = jnp.take(keys.reshape(total_sel, KVH, HS), groups, axis=1)
    values_h = jnp.take(values.reshape(total_sel, KVH, HS), groups, axis=1)
    scores = jnp.einsum(
        "qhd,khd->hqk", query_h, keys_h, preferred_element_type=jnp.float32
    ) / jnp.sqrt(jnp.float32(HS))
    causal = jnp.arange(total_sel)[:, None] >= jnp.arange(total_sel)[None, :]
    scores = jnp.where(causal[None], scores, jnp.float32(-1e30))
    top = jnp.max(scores, axis=2, keepdims=True)
    weights = jnp.exp(scores - top)
    probs = (weights / jnp.sum(weights, axis=2, keepdims=True)).astype(jnp.bfloat16)
    attended = jnp.einsum(
        "hqk,khd->qhd", probs, values_h, preferred_element_type=jnp.float32
    ).astype(jnp.bfloat16)
    attended = attended.reshape(total_sel, heads_here * HS)
    dealt = (
        attended.reshape(per_dev, devices, heads_here * HS)
        .transpose(1, 0, 2)
        .reshape(total_sel, heads_here * HS)
    )
    update = lax.psum_scatter(
        jnp.dot(dealt, w_out, preferred_element_type=jnp.float32).astype(jnp.bfloat16),
        "ctx",
        scatter_dimension=0,
        tiled=True,
    ).astype(jnp.float32)
    own_rows = jnp.take(routed.reshape(per_dev, devices, width), myself, axis=1)
    gate = jax.nn.sigmoid(jnp.dot(own_rows, router, preferred_element_type=jnp.float32))
    fresh = (own_rows.astype(jnp.float32) + gate[:, None] * update).astype(jnp.bfloat16)
    route_back = jnp.arange(devices, dtype=jnp.int32)[:, None] == my_owner[None, :]
    outgoing_back = jnp.where(route_back[:, :, None], fresh[None, :, :], jnp.zeros((), fresh.dtype))
    returned = lax.all_to_all(
        outgoing_back, "ctx", split_axis=0, concat_axis=0, tiled=True
    ).reshape(total_sel, width)
    target = jnp.where(owner == myself, selected - myself * tok_dev, tok_dev)
    target_dealt = target.reshape(per_dev, devices).transpose(1, 0).reshape(total_sel)
    return tokens.at[target_dealt].set(returned, mode="drop")


def solution(mesh):
    placed = (
        P(("dp", "ctx"), None),
        P("dp"),
        P(),
        P(),
        P(None, "ctx"),
        P(None, "ctx"),
        P(None, "ctx"),
        P("ctx", None),
    )
    return jax.shard_map(
        on_device, mesh=mesh, in_specs=placed, out_specs=P(("dp", "ctx"), None), check_vma=False
    )
```

profile of v0, /device:TPU:480, one launch (start us, length us, event | category | flops | bytes accessed | tf_op | source)
XLA Modules:
  0.0 305.1 jit_solution(6910555682631366388)
XLA Ops:
  6.5 1.3 copy.49
  8.1 0.8 fusion.30
  9.4 9.9 %compare_select_fusion.1 = (s32[256]{0:T(256)S(1)}, s32[256]{0:T(256)S(1)}, f32[256]{0:T(256)S(1)}) fusion(s32[]{:T(128)} %bitcast.3, s32[]{:T(128)} %bitcast.4, s32[]{:T(128)} %bitcast.5, s32[]{:T(128)} %bitcast.6, s32[]{:T(128)} %bitcast.7, s32[]{:T(128)} %bitcast.8, s32[]{:T(128)} %bitcast.9, s32[]{:T(128)} %bitcast.10, s32[]{:T(128)} %bitcast.11, ...), kind=kLoop, calls=%fused_computation.58 | loop fusion | flops 14080 | bytes 4160 | tf_op jit(solution)/shard_map/select_n | solution.py:52
  19.4 0.6 convert_reduce_fusion.1
  20.0 0.6 iota_compare_fusion.2
  20.6 0.6 compare_select_fusion.3
  21.2 0.7 gather_fusion
  21.9 0.8 broadcast_select_fusion.1
  23.3 0.3 broadcast_multiply_fusion
  23.6 65.1 %all-gather.2.cloned.1.call-done = bf16[512,4096]{1,0:T(8,128)(2,1)} async-done(((bf16[32,4096]{1,0:T(8,128)(2,1)}), bf16[512,4096]{1,0:T(8,128)(2,1)}) %all-gather.2.cloned.1.call-update) | async-done | bytes 4194320 | tf_op jit(solution)/shard_map/all_gather | solution.py:50
  88.8 7.9 %gather_fusion.1 = bf16[256,4096]{1,0:T(8,128)(2,1)} fusion(bf16[512,4096]{1,0:T(8,128)(2,1)} %all-gather.2.cloned.1.call-done, s32[1024]{0:T(1024)S(1)} %pad_clamp_fusion), kind=kCustom, calls=%fused_computation.1 | custom fusion | bytes 4195328 | tf_op jit(solution)/shard_map/gather | solution.py:52
  96.7 2.2 fusion
  99.0 0.6 fusion.2
  99.6 1.3 copy-done.2
  101.0 0.7 fusion.34
  101.7 23.6 %all_gather.11 = f32[256,512]{0,1:T(8,128)S(1)} all-gather(f32[256,32]{0,1:T(8,128)S(1)} %fusion.34), channel_id=1, replica_groups=mesh['dp'=32,'ctx'=16] {'ctx'}, dimensions={1}, use_global_device_ids=true | all-gather | bytes 557056 | tf_op jit(solution)/shard_map/all_gather | solution.py:62
  125.5 0.3 reshape_reshape.6
  125.9 8.0 %subtract_convert_fusion = (bf16[256,256,1]{0,2,1:T(2,128)(2,1)S(1)}, bf16[256,256,1]{0,2,1:T(2,128)(2,1)S(1)}) fusion(f32[256,256,2]{0,2,1:T(2,128)S(1)} %reshape_reshape.6, f32[256,256,2]{0,2,1:T(2,128)S(1)} %broadcast_multiply_fusion), kind=kLoop, calls=%fused_computation.25 | loop fusion | flops 524288 | bytes 1048576 | tf_op jit(solution)/shard_map/convert
  133.9 0.6 pad_maximum_fusion
  134.6 2.7 fusion.33
  137.4 2.1 subtract_convert_fusion.1
  139.7 2.3 fusion.32
  142.0 21.7 %all_gather.10 = bf16[256,512]{0,1:T(8,128)(2,1)S(1)} all-gather(bf16[256,32]{0,1:T(8,128)(2,1)S(1)} %fusion.32), channel_id=1, replica_groups=mesh['dp'=32,'ctx'=16] {'ctx'}, dimensions={1}, use_global_device_ids=true | all-gather | bytes 278528 | tf_op jit(solution)/shard_map/all_gather | solution.py:63
  164.8 2.0 convolution_convert_fusion
  167.1 1.5 constant_dynamic-slice_fusion
  168.7 0.3 fusion.8
  169.0 87.2 %reduce-scatter.2.cloned.1.call-done = bf16[16,4096]{1,0:T(8,128)(2,1)} async-done(((bf16[256,4096]{1,0:T(8,128)(2,1)}), bf16[16,4096]{1,0:T(8,128)(2,1)}) %reduce-scatter.2.cloned.1.call-update) | async-done | bytes 131088 | tf_op jit(solution)/shard_map/reduce_scatter | solution.py:89
  256.2 1.1 add_convert_fusion
  257.2 1.5 broadcast_select_fusion
  258.7 4.9 %all-to-all-start = ((bf16[16,16,4096]{2,1,0:T(8,128)(2,1)}), bf16[16,16,4096]{2,1,0:T(8,128)(2,1)}, u32[]{:S(2)}, u32[]{:S(2)}) async-start(bf16[16,16,4096]{2,1,0:T(8,128)(2,1)} %broadcast_select_fusion), calls=%async_computation.1 | async-start | bytes 4194304 | tf_op jit(solution)/shard_map/all_to_all | solution.py:100
  263.9 27.8 %all-to-all-done = bf16[16,16,4096]{2,1,0:T(8,128)(2,1)} async-done(((bf16[16,16,4096]{2,1,0:T(8,128)(2,1)}), bf16[16,16,4096]{2,1,0:T(8,128)(2,1)}, u32[]{:S(2)}, u32[]{:S(2)}) %all-to-all-start) | async-done | bytes 2097184 | tf_op jit(solution)/shard_map/all_to_all | solution.py:100
  291.7 6.6 %scatter_fusion = bf16[128,4096]{1,0:T(8,128)(2,1)} fusion(bf16[128,4096]{1,0:T(8,128)(2,1)} %copy-done.1, s32[256]{0:T(256)S(1)} %bitcast.90, bf16[256,4096]{1,0:T(8,128)(2,1)} %bitcast.36), kind=kCustom, calls=%fused_computation.2 | custom fusion | bytes 6292480 | tf_op jit(solution)/shard_map/scatter | solution.py:105
  (53 shorter events, 2.8 us)
Async XLA Ops:
  6.5 158.2 %copy-start = (bf16[128,4096]{1,0:T(8,128)(2,1)S(1)}, bf16[128,4096]{1,0:T(8,128)(2,1)}, u32[]{:S(2)}) copy-start(bf16[128,4096]{1,0:T(8,128)(2,1)} %param.17) | copy-start | bytes 3145732
  6.5 1.3 copy-start.6
  6.5 82.2 %all-gather.2.cloned.1.call-start = ((), (), s32[]{:S(2)}) async-start(), calls=%async_computation.2 | async-start | bytes 4456448 | tf_op jit(solution)/shard_map/all_gather | solution.py:50
  7.9 15.8 %copy-start.1 = (bf16[128,4096]{1,0:T(8,128)(2,1)}, bf16[128,4096]{1,0:T(8,128)(2,1)S(1)}, u32[]{:S(2)}) copy-start(bf16[128,4096]{1,0:T(8,128)(2,1)S(1)} %copy.49) | copy-start | bytes 3145732
  7.9 15.0 %copy-start.7 = (bf16[4096]{0:T(1024)(128)(2,1)S(1)}, bf16[4096]{0:T(1024)(128)(2,1)}, u32[]{:S(2)}) copy-start(bf16[4096]{0:T(1024)(128)(2,1)} %param.12) | copy-start | bytes 24580
  22.7 233.4 %reduce-scatter.2.cloned.1.call-start = ((), (), s32[]{:S(2)}) async-start(), calls=%async_computation.3 | async-start | bytes 2228224 | tf_op jit(solution)/shard_map/reduce_scatter | solution.py:89
  96.7 2.2 copy-start.3
  99.0 2.0 copy-start.4
  99.6 1.3 copy-start.2
  134.6 5.1 %copy-start.5 = (bf16[4096,32]{0,1:T(8,128)(2,1)S(1)}, bf16[4096,32]{0,1:T(8,128)(2,1)}, u32[]{:S(2)}) copy-start(bf16[4096,32]{0,1:T(8,128)(2,1)} %param.16) | copy-start | bytes 786436
  164.8 2.2 copy-start.8
  258.7 32.9 %all-to-all-start = ((bf16[16,16,4096]{2,1,0:T(8,128)(2,1)}), bf16[16,16,4096]{2,1,0:T(8,128)(2,1)}, u32[]{:S(2)}, u32[]{:S(2)}) async-start(bf16[16,16,4096]{2,1,0:T(8,128)(2,1)} %broadcast_select_fusion), calls=%async_computation.1 | async-start | bytes 4194304 | tf_op jit(solution)/shard_map/all_to_all | solution.py:100
Sparse Core Ops, SparseCore 0:
  22.9 65.8 all-gather.1
  167.0 89.1 reduce-scatter.1
where the time goes:
time: 311 us; the launch traced here: 305 us
  waiting for transfers between devices  180 us (58%)
  blocking collectives  45.3 us (15%)
  other arithmetic  29.9 us (10%)
  local copies, waits for them, and re-layouts  22 us (7%)
  between operations  14.3 us (5%)
  matrix products  8.52 us (3%)
  starting transfers between devices  4.93 us (2%)
    reduce_scatter x1, waiting for transfers between devices, on_device(): lax.psum_scatter(jnp.dot(dealt, w_out, preferred_element_type=jnp.float32...  87.2 us
    all_gather x1, waiting for transfers between devices, on_device(): gathered = lax.all_gather(packed, 'ctx', axis=0, tiled=True)  65.1 us
    all_to_all x1, waiting for transfers between devices, on_device(): lax.all_to_all(outgoing_back, 'ctx', split_axis=0, concat_axis=0, tiled=T...  27.8 us
    all_gather x1, blocking collectives, on_device(): lax.all_gather(key_part, 'ctx', axis=1, tiled=True)  23.6 us
    all_gather x1, blocking collectives, on_device(): lax.all_gather(value_part, 'ctx', axis=1, tiled=True)  21.7 us
    another operation x2, other arithmetic  10.1 us
    select_n x1, other arithmetic, on_device(): routed = gathered[source]  9.94 us
    gather x1, local copies, waits for them, and re-layouts, on_device(): routed = gathered[source]  7.93 us
  transfers between devices with their start and end apart: 3, of which 3 were waited for; matrix products, arithmetic and copies ran while one was open for 1% of the time, Pallas kernels for 0%

commit v1 on v0

v1 whole, which is shorter than its diff:
```python
import jax
import jax.numpy as jnp
from jax import lax
from jax.experimental import pallas as pl
from jax.experimental.pallas import tpu as pltpu
from jax.sharding import PartitionSpec as P

HS = 128
HQ = 16
KVH = 4
CAP = 32
N = 16
TOK = 128
SEL = 256
D = 4096
SL = D // N
BF = jnp.bfloat16
F32 = jnp.float32
NT = (((1,), (1,)), ((), ()))
CHUNK = SEL + SEL // 2


def one_hot(mask):
    return jnp.where(mask, 1.0, 0.0).astype(BF)


def slots(sel, me):
    base = me * TOK
    first = jnp.sum(jnp.where(sel < base, 1.0, 0.0), axis=1, keepdims=True).astype(jnp.int32)
    mine = (sel >= base) & (sel < base + TOK)
    rank = lax.broadcasted_iota(jnp.int32, (CAP, SEL), 1)
    slot = lax.broadcasted_iota(jnp.int32, (CAP, SEL), 0)
    by_slot = one_hot((rank - first == slot) & mine)
    token = lax.broadcasted_iota(jnp.int32, (TOK, SEL), 0)
    by_token = one_hot(token + base == sel)
    return by_slot, by_token


def pack_kernel(sel_ref, tok_ref, gain_ref, router_ref, wout_ref, send_ref, raw_ref, gate_ref):
    by_slot, by_token = slots(sel_ref[...], lax.axis_index("ctx"))
    pick = lax.dot_general(by_slot, by_token, NT, preferred_element_type=F32).astype(BF)
    raw = jnp.dot(pick, tok_ref[...], preferred_element_type=F32)
    raw_ref[...] = raw.astype(BF)
    scale = lax.rsqrt(jnp.mean(raw * raw, axis=1, keepdims=True) + 1e-05)
    normed = (raw * scale * gain_ref[...].astype(F32)).astype(BF)
    logit = jnp.sum(raw * router_ref[...].astype(F32), axis=1, keepdims=True)
    gate_ref[...] = jnp.broadcast_to(1.0 / (1.0 + jnp.exp(-logit)), (CAP, 128))
    for c in range(N):
        send_ref[c, :CAP, :] = normed[:, c * SL : (c + 1) * SL]
        send_ref[c, CAP:, :] = wout_ref[:, c * SL : (c + 1) * SL]


def compact_kernel(sel_row_ref, sel_col_ref, recv_ref, out_ref):
    sel_row, sel_col = sel_row_ref[...], sel_col_ref[...]
    owner = sel_col >> 7
    first = jnp.sum(jnp.where(sel_row < owner * TOK, 1.0, 0.0), axis=1, keepdims=True).astype(jnp.int32)
    place = owner * CAP + lax.broadcasted_iota(jnp.int32, (SEL, 1), 0) - first
    pick = one_hot(lax.broadcasted_iota(jnp.int32, (SEL, N * CAP), 1) == place)
    rows = recv_ref[:, :CAP, :].reshape(N * CAP, SL)
    dense = jnp.dot(pick, rows, preferred_element_type=F32).astype(BF)
    for d in range(N):
        out_ref[d] = dense


def qkv_kernel(x_ref, w_ref, cos_ref, sin_ref, out_ref):
    acc = jnp.zeros((SEL, 256), F32)
    for f in range(N):
        acc += jnp.dot(x_ref[f], w_ref[f * SL : (f + 1) * SL, :], preferred_element_type=F32)
    lane = lax.broadcasted_iota(jnp.int32, (SEL, 128), 1)
    q, kv = acc[:, :128], acc[:, 128:]
    q_mate = jnp.where(lane % 2 == 0, pltpu.roll(q, 127, 1), pltpu.roll(q, 1, 1))
    q = (q * cos_ref[:, :128] + q_mate * sin_ref[:, :128]).astype(BF)
    kv_mate = jnp.where(lane % 8 < 4, pltpu.roll(kv, 124, 1), pltpu.roll(kv, 4, 1))
    kv = (kv * cos_ref[:, 128:] + kv_mate * sin_ref[:, 128:]).astype(BF)
    to = lax.broadcasted_iota(jnp.int32, (64, 128), 0)
    frm = lax.broadcasted_iota(jnp.int32, (64, 128), 1)
    order = one_hot(frm == ((to >> 3) & 1) * 32 + (to & 7) * 4 + (to >> 4))
    turned = lax.dot_general(order, kv, NT, preferred_element_type=F32).astype(BF)
    for d in range(N):
        out_ref[d, :SEL, :] = q
        out_ref[d, SEL : SEL + 64, :] = turned[:, :128]
        out_ref[d, SEL + 64 :, :] = turned[:, 128:]


def attend_kernel(sel_row_ref, sel_col_ref, recv_ref, wout_ref, out_ref):
    left = recv_ref[:, SEL : SEL + 64, :].astype(F32).reshape(N, KVH, 2, 8, 128)
    right = recv_ref[:, SEL + 64 :, :].astype(F32).reshape(N, KVH, 2, 8, 128)
    row = lax.broadcasted_iota(jnp.int32, (SEL, SEL), 0)
    col = lax.broadcasted_iota(jnp.int32, (SEL, SEL), 1)
    causal = row >= col
    acc = jnp.zeros((SEL, SL), F32)
    for g in range(KVH):
        keys, values = [
            jnp.concatenate([half[:, g, i].reshape(HS, 128) for half in (left, right)], axis=1).astype(BF)
            for i in range(2)
        ]
        for h in range(g * HQ // KVH, (g + 1) * HQ // KVH):
            scores = jnp.dot(recv_ref[h, :SEL, :], keys, preferred_element_type=F32) * (HS**-0.5)
            scores = jnp.where(causal, scores, -1e30)
            weights = jnp.exp(scores - jnp.max(scores, axis=1, keepdims=True))
            probs = (weights / jnp.sum(weights, axis=1, keepdims=True)).astype(BF)
            mixed = lax.dot_general(probs, values, NT, preferred_element_type=F32).astype(BF)
            acc += jnp.dot(mixed, wout_ref[h, CAP:, :], preferred_element_type=F32)
    sel_row, sel_col = sel_row_ref[...], sel_col_ref[...]
    owner = sel_row >> 7
    first = jnp.sum(jnp.where(sel_col < owner * TOK, 1.0, 0.0), axis=0, keepdims=True).astype(jnp.int32)
    place = owner * CAP + lax.broadcasted_iota(jnp.int32, (1, SEL), 1) - first
    put = one_hot(lax.broadcasted_iota(jnp.int32, (N * CAP, SEL), 0) == place)
    sent = jnp.dot(put, acc.astype(BF), preferred_element_type=F32).astype(BF)
    out_ref[...] = sent.reshape(N, CAP, SL)


def finish_kernel(sel_ref, tok_ref, raw_ref, gate_ref, recv_ref, out_ref):
    by_slot, by_token = slots(sel_ref[...], lax.axis_index("ctx"))
    put = lax.dot_general(by_token, by_slot, NT, preferred_element_type=F32).astype(BF)
    live = jnp.sum(by_token.astype(F32), axis=1, keepdims=True) > 0.5
    gate = gate_ref[:, :1]
    for c in range(N):
        part = slice(c * SL, (c + 1) * SL)
        fresh = (raw_ref[:, part].astype(F32) + gate * recv_ref[c].astype(F32)).astype(BF)
        placed = jnp.dot(put, fresh, preferred_element_type=F32).astype(BF)
        out_ref[:, part] = jnp.where(live, placed, tok_ref[:, part])


def call(kernel, shapes, n_in, flops, moved, name):
    return pl.pallas_call(
        kernel,
        out_shape=shapes,
        in_specs=[pl.BlockSpec(memory_space=pltpu.VMEM)] * n_in,
        out_specs=jax.tree.map(lambda _: pl.BlockSpec(memory_space=pltpu.VMEM), shapes),
        compiler_params=pltpu.CompilerParams(vmem_limit_bytes=40 * 1024 * 1024),
        cost_estimate=pl.CostEstimate(flops=flops, bytes_accessed=moved, transcendentals=0),
        name=name,
    )


def on_device(tokens, selected, norm_gain, router, w_query, w_key, w_value, w_out):
    me = lax.axis_index("ctx")
    shape = jax.ShapeDtypeStruct
    sel_row, sel_col = selected.reshape(1, SEL), selected.reshape(SEL, 1)
    send, raw, gate = call(
        pack_kernel,
        (shape((N, CAP + TOK, SL), BF), shape((CAP, D), BF), shape((CAP, 128), F32)),
        5, 2 * CAP * TOK * D, 4 << 20, "pack",
    )(sel_row, tokens, norm_gain.reshape(1, D), router.reshape(1, D), w_out)
    got = lax.all_to_all(send, "ctx", 0, 0, tiled=True)
    weights = jnp.concatenate([w_query, w_key, w_value, jnp.zeros((D, 64), BF)], axis=1)
    lane = jnp.arange(256)
    component = jnp.where(lane < HS, lane, me * 8 + (lane - HS) // 4)
    pair = (component // 2).astype(F32)
    inverse = jnp.exp(-(2.0 * pair / HS) * jnp.log(10000.0))
    inverse = jnp.where(lane < HS + 32, inverse, 0.0)
    angle = selected.astype(F32)[:, None] * inverse[None, :]
    cosine = jnp.cos(angle)
    sine = jnp.sin(angle) * jnp.where(component % 2 == 0, -1.0, 1.0)[None, :]
    copies = call(compact_kernel, shape((N, SEL, SL), BF), 3, 2 * SEL * 512 * SL, 4 << 20, "compact")(
        sel_row, sel_col, got
    )
    rows = lax.all_to_all(copies, "ctx", 0, 0, tiled=True)
    qkv = call(qkv_kernel, shape((N, CHUNK, HS), BF), 4, 2 * SEL * D * 256, 6 << 20, "qkv")(
        rows, weights, cosine, sine
    )
    heads = lax.all_to_all(qkv, "ctx", 0, 0, tiled=True)
    update = call(attend_kernel, shape((N, CAP, SL), BF), 4, 2 * 16 * 3 * 256 * 256 * 128, 4 << 20, "attend")(
        sel_row, sel_col, heads, got
    )
    back = lax.all_to_all(update, "ctx", 0, 0, tiled=True)
    return call(finish_kernel, shape((TOK, D), BF), 5, 2 * TOK * CAP * D, 4 << 20, "finish")(
        sel_row, tokens, raw, gate, back
    )


def solution(mesh):
    placed = (
        P(("dp", "ctx"), None),
        P("dp"),
        P(),
        P(),
        P(None, "ctx"),
        P(None, "ctx"),
        P(None, "ctx"),
        P("ctx", None),
    )
    return jax.shard_map(
        on_device, mesh=mesh, in_specs=placed, out_specs=P(("dp", "ctx"), None), check_vma=False
    )
```

time: 311 us -> 116 us (0.37); the launches traced: 305 us -> 116 us
  waiting for transfers between devices: 180 us -> 38.1 us
  other arithmetic: 29.9 us -> 5.8 us
  between operations: 14.3 us -> 0.11 us
  Pallas kernels: 0 us -> 9.57 us
  blocking collectives: 45.3 us -> 36 us
  matrix products: 8.52 us -> 0 us
  local copies, waits for them, and re-layouts: 22 us -> 15.4 us
  starting transfers between devices: 4.93 us -> 10.8 us
    reduce_scatter x1 -> x0, waiting for transfers between devices: 87.2 us -> none  [on_device(): lax.psum_scatter(jnp.dot(dealt, w_out, preferred_element_type=jnp.float32...]
    all_gather x1 -> x0, waiting for transfers between devices: 65.1 us -> none  [on_device(): gathered = lax.all_gather(packed, 'ctx', axis=0, tiled=True)]
    all_gather x2 -> x0, blocking collectives: 45.3 us -> none  [the longest x1 23.6 us: on_device(): lax.all_gather(key_part, 'ctx', axis=1, tiled=True)]
    all_to_all x0 -> x2, blocking collectives: none -> 36 us  [the longest x1 24.3 us: on_device(): heads = lax.all_to_all(qkv, 'ctx', 0, 0, tiled=True)]
    select_n x6 -> x1, other arithmetic: 13.1 us -> 0.03 us  [on_device(): sine = jnp.sin(angle) * jnp.where(component % 2 == 0, -1.0, 1.0)[None, :]]
    unnamed x20 -> x28, local copies, waits for them, and re-layouts: 2.71 us -> 13.8 us
    another operation x4 -> x0, other arithmetic: 10.9 us -> none
    all_to_all x1 -> x2, waiting for transfers between devices: 27.8 us -> 38.1 us  [the longest x1 20.6 us: on_device(): got = lax.all_to_all(send, 'ctx', 0, 0, tiled=True)]
  transfers between devices with their start and end apart: 3 -> 2, of which waited for: 3 -> 2; matrix products, arithmetic and copies ran while one was open for 1% -> 9% of each run, Pallas kernels for 0% -> 0%
where the time goes in v1:
time: 116 us
  waiting for transfers between devices  38.1 us (33%)
  blocking collectives  36 us (31%)
  local copies, waits for them, and re-layouts  15.4 us (13%)
  starting transfers between devices  10.8 us (9%)
  Pallas kernels  9.57 us (8%)
  other arithmetic  5.8 us (5%)
    all_to_all x1, blocking collectives, on_device(): heads = lax.all_to_all(qkv, 'ctx', 0, 0, tiled=True)  24.3 us
    all_to_all x1, waiting for transfers between devices, on_device(): got = lax.all_to_all(send, 'ctx', 0, 0, tiled=True)  20.6 us
    all_to_all x1, waiting for transfers between devices, on_device(): rows = lax.all_to_all(copies, 'ctx', 0, 0, tiled=True)  17.5 us
    unnamed x28, local copies, waits for them, and re-layouts  13.8 us
    all_to_all x1, blocking collectives, on_device(): back = lax.all_to_all(update, 'ctx', 0, 0, tiled=True)  11.7 us
    all_to_all x1, starting transfers between devices, on_device(): got = lax.all_to_all(send, 'ctx', 0, 0, tiled=True)  7.03 us
    pallas_call x1, Pallas kernels, on_device(): call(attend_kernel, shape((N, CAP, SL), BF), 4, 2 * 16 * 3 * 256 * 256 *...  4.55 us
    concatenate x1, other arithmetic, on_device(): jnp.concatenate([w_query, w_key, w_value, jnp.zeros((D, 64), BF)], axis=1)  3.95 us
  transfers between devices with their start and end apart: 2, of which 2 were waited for; matrix products, arithmetic and copies ran while one was open for 9% of the time, Pallas kernels for 0%

profile of v1, /device:TPU:480, one launch (start us, length us, event | category | flops | bytes accessed | tf_op | source)
XLA Modules:
  0.0 115.8 jit_solution(194688295418884019)
XLA Ops:
  0.0 0.7 reshape.76.gain_ref
  0.7 0.7 reshape.77.router_ref
  1.4 0.0 copy-start.2
  1.4 1.2 %copy-done.2 = bf16[128,4096]{1,0:T(8,128)(2,1)S(1)} copy-done((bf16[128,4096]{1,0:T(8,128)(2,1)S(1)}, bf16[128,4096]{1,0:T(8,128)(2,1)}, u32[]{:S(2)}) %copy-start.2) | copy-done | bytes 1048600
  2.7 1.2 %copy-done.6 = bf16[128,4096]{1,0:T(8,128)(2,1)S(1)} copy-done((bf16[128,4096]{1,0:T(8,128)(2,1)S(1)}, bf16[128,4096]{1,0:T(8,128)(2,1)}, u32[]{:S(2)}) %copy-start.6) | copy-done | bytes 1048600
  3.9 0.7 copy-done.9
  4.6 1.8 %pack.1 = (bf16[16,160,256]{2,1,0:T(8,128)(2,1)}, bf16[32,4096]{1,0:T(8,128)(2,1)S(1)}, f32[32,128]{1,0:T(8,128)S(1)}) custom-call(s32[1,256]{1,0:T(1,128)S(1)} %bitcast.2, bf16[128,4096]{1,0:T(8,128)(2,1)S(1)} %copy-done.2, bf16[1,4096]{1,0:T(2,128)(2,1)S(1)} %reshape.76.gain_ref, bf16[1,4096]{1,0:T(2,128)(2,1)S(1)} %reshape.77.router_ref, ...), custom_call_target="tpu_custom_call" | custom-call | flops 33554432 | bytes 4194304 | tf_op jit(solution)/shard_map/pack/pallas_call | solution.py:141
  6.3 0.7 copy-done.7
  7.1 0.6 copy-done.11
  7.7 7.0 %all-to-all-start = ((bf16[16,160,256]{2,1,0:T(8,128)(2,1)}), bf16[16,160,256]{2,1,0:T(8,128)(2,1)S(1)}, u32[]{:S(2)}, u32[]{:S(2)}) async-start(bf16[16,160,256]{2,1,0:T(8,128)(2,1)} %get-tuple-element.10), calls=%async_computation | async-start | bytes 2621440 | tf_op jit(solution)/shard_map/all_to_all | solution.py:146
  14.7 0.0 copy-done.10
  14.7 0.1 copy.14.sel_col_ref
  14.8 20.6 %all-to-all-done.recv_ref.wout_ref = bf16[16,160,256]{2,1,0:T(8,128)(2,1)S(1)} async-done(((bf16[16,160,256]{2,1,0:T(8,128)(2,1)}), bf16[16,160,256]{2,1,0:T(8,128)(2,1)S(1)}, u32[]{:S(2)}, u32[]{:S(2)}) %all-to-all-start) | async-done | bytes 1310752 | tf_op jit(solution)/shard_map/all_to_all | solution.py:146
  35.5 0.6 compact.1
  36.1 0.0 copy-start.1
  36.1 1.3 %copy-done.1 = bf16[16,256,256]{2,1,0:T(8,128)(2,1)} copy-done((bf16[16,256,256]{2,1,0:T(8,128)(2,1)}, bf16[16,256,256]{2,1,0:T(8,128)(2,1)S(1)}, u32[]{:S(2)}) %copy-start.1) | copy-done | bytes 2097176
  37.4 3.7 %all-to-all-start.1 = ((bf16[16,256,256]{2,1,0:T(8,128)(2,1)}), bf16[16,256,256]{2,1,0:T(8,128)(2,1)S(1)}, u32[]{:S(2)}, u32[]{:S(2)}) async-start(bf16[16,256,256]{2,1,0:T(8,128)(2,1)} %copy-done.1), calls=%async_computation.1 | async-start | bytes 4194304 | tf_op jit(solution)/shard_map/all_to_all | solution.py:159
  41.2 2.3 %copy.13 = bf16[4096,32]{1,0:T(8,128)(2,1)} copy(bf16[4096,32]{0,1:T(8,128)(2,1)} %param.14) | data formatting | bytes 524288 | tf_op args[6]
  43.5 2.3 %copy.12 = bf16[4096,32]{1,0:T(8,128)(2,1)} copy(bf16[4096,32]{0,1:T(8,128)(2,1)} %param.13) | data formatting | bytes 524288 | tf_op args[5]
  45.7 0.1 pad.3.clone
  45.8 1.8 %fusion = (f32[256,256]{1,0:T(8,128)}, f32[256,256]{1,0:T(8,128)}) fusion(f32[256]{0:T(256)S(1)} %get-tuple-element.13, f32[256]{0:T(256)S(1)} %get-tuple-element.14, f32[256]{0:T(256)S(1)} %convert_element_type.10), kind=kLoop, calls=%fused_computation.3 | loop fusion | flops 131072 | bytes 527360 | tf_op jit(solution)/shard_map/mul | solution.py:155
  47.7 4.0 %maximum_maximum_fusion.w_ref = bf16[4096,256]{1,0:T(8,128)(2,1)} fusion(bf16[4096,32]{1,0:T(8,128)(2,1)} %copy.13, bf16[4096,32]{1,0:T(8,128)(2,1)} %copy.12, bf16[4096,128]{1,0:T(8,128)(2,1)} %param.12, bf16[256]{0:T(256)(128)(2,1)S(1)} %pad.3.clone), kind=kLoop, calls=%fused_computation | loop fusion | flops 8388608 | bytes 3670528 | tf_op jit(solution)/shard_map/concatenate | solution.py:147
  51.6 17.5 %all-to-all-done.1.x_ref = bf16[16,256,256]{2,1,0:T(8,128)(2,1)S(1)} async-done(((bf16[16,256,256]{2,1,0:T(8,128)(2,1)}), bf16[16,256,256]{2,1,0:T(8,128)(2,1)S(1)}, u32[]{:S(2)}, u32[]{:S(2)}) %all-to-all-start.1) | async-done | bytes 2097184 | tf_op jit(solution)/shard_map/all_to_all | solution.py:159
  69.1 1.6 %copy-done = bf16[4096,256]{1,0:T(8,128)(2,1)S(1)} copy-done((bf16[4096,256]{1,0:T(8,128)(2,1)S(1)}, bf16[4096,256]{1,0:T(8,128)(2,1)}, u32[]{:S(2)}) %copy-start) | copy-done | bytes 2097176
  70.7 0.9 copy-done.4
  71.6 0.9 copy-done.5
  72.6 1.0 qkv.1
  73.6 24.3 %all_to_all.20.recv_ref = bf16[16,384,128]{2,1,0:T(8,128)(2,1)S(1)} all-to-all(bf16[16,384,128]{2,1,0:T(8,128)(2,1)S(1)} %qkv.1), channel_id=1, replica_groups=mesh['dp'=32,'ctx'=16] {'ctx'}, dimensions={0} | all-to-all | bytes 3145728 | tf_op jit(solution)/shard_map/all_to_all | solution.py:163
  97.9 4.5 %attend.1 = bf16[16,32,256]{2,1,0:T(8,128)(2,1)S(1)} custom-call(s32[1,256]{1,0:T(1,128)S(1)} %bitcast.5, s32[256,1]{1,0:T(8,128)S(1)} %copy.14.sel_col_ref, bf16[16,384,128]{2,1,0:T(8,128)(2,1)S(1)} %all_to_all.20.recv_ref, bf16[16,160,256]{2,1,0:T(8,128)(2,1)S(1)} %all-to-all-done.recv_ref.wout_ref), custom_call_target="tpu_custom_call" | custom-call | flops 805306368 | bytes 4194304 | tf_op jit(solution)/shard_map/attend/pallas_call | solution.py:164
  102.4 11.7 %all_to_all.21.recv_ref = bf16[16,32,256]{2,1,0:T(8,128)(2,1)S(1)} all-to-all(bf16[16,32,256]{2,1,0:T(8,128)(2,1)S(1)} %attend.1), channel_id=1, replica_groups=mesh['dp'=32,'ctx'=16] {'ctx'}, dimensions={0} | all-to-all | bytes 524288 | tf_op jit(solution)/shard_map/all_to_all | solution.py:167
  114.2 0.0 copy-done.3
  114.2 1.6 %finish.1 = bf16[128,4096]{1,0:T(8,128)(2,1)} custom-call(s32[1,256]{1,0:T(1,128)S(1)} %bitcast.6, bf16[128,4096]{1,0:T(8,128)(2,1)S(1)} %copy-done.3, bf16[32,4096]{1,0:T(8,128)(2,1)S(1)} %copy-done.8, f32[32,128]{1,0:T(8,128)S(1)} %copy-done.12, bf16[16,32,256]{2,1,0:T(8,128)(2,1)S(1)} %all_to_all.21.recv_ref), custom_call_target="tpu_custom_call" | custom-call | flops 33554432 | bytes 4194304 | tf_op jit(solution)/shard_map/finish/pallas_call | solution.py:168
  (16 shorter events, 0.1 us)
Async XLA Ops:
  1.4 1.2 %copy-start.2 = (bf16[128,4096]{1,0:T(8,128)(2,1)S(1)}, bf16[128,4096]{1,0:T(8,128)(2,1)}, u32[]{:S(2)}) copy-start(bf16[128,4096]{1,0:T(8,128)(2,1)} %tok_ref.3) | copy-start | bytes 3145732
  2.7 1.2 %copy-start.6 = (bf16[128,4096]{1,0:T(8,128)(2,1)S(1)}, bf16[128,4096]{1,0:T(8,128)(2,1)}, u32[]{:S(2)}) copy-start(bf16[128,4096]{1,0:T(8,128)(2,1)} %wout_ref.1) | copy-start | bytes 3145732
  3.9 0.7 copy-start.9
  4.6 10.1 %copy-start.10 = (s32[256]{0:T(256)S(1)}, s32[256]{0:T(256)}, u32[]{:S(2)}) copy-start(s32[256]{0:T(256)} %param.9) | copy-start | bytes 3076
  6.3 0.7 copy-start.7
  7.1 0.6 copy-start.11
  7.7 27.8 %all-to-all-start = ((bf16[16,160,256]{2,1,0:T(8,128)(2,1)}), bf16[16,160,256]{2,1,0:T(8,128)(2,1)S(1)}, u32[]{:S(2)}, u32[]{:S(2)}) async-start(bf16[16,160,256]{2,1,0:T(8,128)(2,1)} %get-tuple-element.10), calls=%async_computation | async-start | bytes 2621440 | tf_op jit(solution)/shard_map/all_to_all | solution.py:146
  36.1 1.3 %copy-start.1 = (bf16[16,256,256]{2,1,0:T(8,128)(2,1)}, bf16[16,256,256]{2,1,0:T(8,128)(2,1)S(1)}, u32[]{:S(2)}) copy-start(bf16[16,256,256]{2,1,0:T(8,128)(2,1)S(1)} %compact.1) | copy-start | bytes 6291460
  37.4 31.6 %all-to-all-start.1 = ((bf16[16,256,256]{2,1,0:T(8,128)(2,1)}), bf16[16,256,256]{2,1,0:T(8,128)(2,1)S(1)}, u32[]{:S(2)}, u32[]{:S(2)}) async-start(bf16[16,256,256]{2,1,0:T(8,128)(2,1)} %copy-done.1), calls=%async_computation.1 | async-start | bytes 4194304 | tf_op jit(solution)/shard_map/all_to_all | solution.py:159
  69.1 1.6 %copy-start = (bf16[4096,256]{1,0:T(8,128)(2,1)S(1)}, bf16[4096,256]{1,0:T(8,128)(2,1)}, u32[]{:S(2)}) copy-start(bf16[4096,256]{1,0:T(8,128)(2,1)} %maximum_maximum_fusion.w_ref) | copy-start | bytes 6291460
  70.7 0.9 copy-start.4
  71.6 0.9 copy-start.5
  97.9 16.3 %copy-start.3 = (bf16[128,4096]{1,0:T(8,128)(2,1)S(1)}, bf16[128,4096]{1,0:T(8,128)(2,1)}, u32[]{:S(2)}) copy-start(bf16[128,4096]{1,0:T(8,128)(2,1)} %tok_ref.3) | copy-start | bytes 3145732
  97.9 16.3 %copy-start.8 = (bf16[32,4096]{1,0:T(8,128)(2,1)S(1)}, bf16[32,4096]{1,0:T(8,128)(2,1)}, u32[]{:S(2)}) copy-start(bf16[32,4096]{1,0:T(8,128)(2,1)} %copy-done.7) | copy-start | bytes 786436
  97.9 16.3 %copy-start.12 = (f32[32,128]{1,0:T(8,128)S(1)}, f32[32,128]{1,0:T(8,128)}, u32[]{:S(2)}) copy-start(f32[32,128]{1,0:T(8,128)} %copy-done.11) | copy-start | bytes 49156

commit v2 on v1

v2 whole, which is shorter than its diff:
```python
import jax
import jax.numpy as jnp
from jax import lax
from jax.experimental import pallas as pl
from jax.experimental.pallas import tpu as pltpu
from jax.sharding import Mesh
from jax.sharding import PartitionSpec as P

HS = 128
HQ = 16
KVH = 4
CAP = 32
N = 16
TOK = 128
SEL = 256
D = 4096
SL = D // N
NZ = 16
BF = jnp.bfloat16
F32 = jnp.float32
NT = (((1,), (1,)), ((), ()))
CHUNK = SEL + SEL // 2
PIECE = 16
VMEM = pltpu.VMEM


def one_hot(mask):
    return jnp.where(mask, 1.0, 0.0).astype(BF)


def slots(sel, me):
    base = me * TOK
    first = jnp.sum(jnp.where(sel < base, 1.0, 0.0), axis=1, keepdims=True).astype(jnp.int32)
    mine = (sel >= base) & (sel < base + TOK)
    rank = lax.broadcasted_iota(jnp.int32, (CAP, SEL), 1)
    slot = lax.broadcasted_iota(jnp.int32, (CAP, SEL), 0)
    by_slot = one_hot((rank - first == slot) & mine)
    token = lax.broadcasted_iota(jnp.int32, (TOK, SEL), 0)
    by_token = one_hot(token + base == sel)
    return by_slot, by_token


def column(row):
    same = lax.broadcasted_iota(jnp.int32, (SEL, SEL), 0) == lax.broadcasted_iota(jnp.int32, (SEL, SEL), 1)
    return jnp.sum(jnp.where(same, row.astype(F32), 0.0), axis=1, keepdims=True).astype(jnp.int32)


def pack_kernel(sel_ref, tok_hbm, gain_ref, wout_hbm, send_ref, tok_ref, wout_ref, sems):
    z, me = lax.axis_index("z"), lax.axis_index("ctx")
    parts = 4
    height = TOK // parts
    loads = [
        pltpu.make_async_copy(
            tok_hbm.at[pl.ds(i * height, height)], tok_ref.at[pl.ds(i * height, height)], sems.at[i]
        )
        for i in range(parts)
    ]
    loads.append(
        pltpu.make_async_copy(
            wout_hbm.at[pl.ds(pl.multiple_of((z // 2) * PIECE, PIECE), PIECE)], wout_ref, sems.at[parts]
        )
    )
    for load in loads:
        load.start()
    by_slot, by_token = slots(sel_ref[...], me)
    pick = lax.dot_general(by_slot, by_token, NT, preferred_element_type=F32).astype(BF)
    for load in loads:
        load.wait()
    raw = jnp.dot(pick, tok_ref[...], preferred_element_type=F32)
    scale = lax.rsqrt(jnp.mean(raw * raw, axis=1, keepdims=True) + 1e-05)
    normed = (raw * scale * gain_ref[...].reshape(1, D).astype(F32)).astype(BF)
    right = z % 2 == 1
    for c in range(N):
        send_ref[c, :CAP, :] = normed[:, c * SL : c * SL + 128]
        send_ref[c, CAP : 2 * CAP, :] = normed[:, c * SL + 128 : (c + 1) * SL]
        send_ref[c, 2 * CAP :, :] = jnp.where(
            right, wout_ref[:, c * SL + 128 : (c + 1) * SL], wout_ref[:, c * SL : c * SL + 128]
        )


def compact_kernel(sel_ref, recv_ref, out_ref, piece_ref):
    sel_row = sel_ref[...]
    owner = column(sel_row) >> 7
    first = jnp.sum(jnp.where(sel_row < owner * TOK, 1.0, 0.0), axis=1, keepdims=True).astype(jnp.int32)
    place = owner * CAP + lax.broadcasted_iota(jnp.int32, (SEL, 1), 0) - first
    pick = one_hot(lax.broadcasted_iota(jnp.int32, (SEL, N * CAP), 1) == place)
    left = jnp.dot(pick, recv_ref[:, :CAP, :].reshape(N * CAP, 128), preferred_element_type=F32)
    right = jnp.dot(pick, recv_ref[:, CAP : 2 * CAP, :].reshape(N * CAP, 128), preferred_element_type=F32)
    dense = jnp.concatenate([left, right], axis=1).astype(BF)
    for d in range(N):
        out_ref[d] = dense
        piece_ref[d * PIECE : (d + 1) * PIECE, :] = recv_ref[d, 2 * CAP :, :]


def qkv_kernel(x_ref, wq_ref, wk_ref, wv_ref, qcos_ref, qsin_ref, kcos_ref, ksin_ref, out_ref):
    q = jnp.zeros((SEL, HS), F32)
    kv = jnp.zeros((SEL, 64), F32)
    for f in range(N):
        part = slice(f * SL, (f + 1) * SL)
        q += jnp.dot(x_ref[f], wq_ref[part, :], preferred_element_type=F32)
        both = jnp.concatenate([wk_ref[:, part], wv_ref[:, part]], axis=0)
        kv += lax.dot_general(x_ref[f], both, NT, preferred_element_type=F32)
    lane = lax.broadcasted_iota(jnp.int32, (SEL, 128), 1)
    q_mate = jnp.where(lane % 2 == 0, pltpu.roll(q, 127, 1), pltpu.roll(q, 1, 1))
    q = (q * qcos_ref[...] + q_mate * qsin_ref[...]).astype(BF)
    kv = jnp.concatenate([kv, kv], axis=1)
    kv_mate = jnp.where(lane % 8 < 4, pltpu.roll(kv, 124, 1), pltpu.roll(kv, 4, 1))
    kv = (kv * kcos_ref[...] + kv_mate * ksin_ref[...]).astype(BF)
    to = lax.broadcasted_iota(jnp.int32, (64, 128), 0)
    frm = lax.broadcasted_iota(jnp.int32, (64, 128), 1)
    order = one_hot(frm == ((to >> 3) & 1) * 32 + (to & 7) * 4 + (to >> 4))
    turned = lax.dot_general(order, kv, NT, preferred_element_type=F32).astype(BF)
    for d in range(N):
        out_ref[d, :SEL, :] = q
        out_ref[d, SEL : SEL + 64, :] = turned[:, :128]
        out_ref[d, SEL + 64 :, :] = turned[:, 128:]


def attend_kernel(sel_ref, recv_ref, wout_hbm, out_ref, wout_ref, mixed_ref, sems):
    parts = 4
    height = NZ * N * PIECE // parts
    loads = [
        pltpu.make_async_copy(
            wout_hbm.at[pl.ds(i * height, height)], wout_ref.at[pl.ds(i * height, height)], sems.at[i]
        )
        for i in range(parts)
    ]
    for load in loads:
        load.start()
    half = SEL // 2
    left = recv_ref[:, SEL : SEL + 64, :].astype(F32).reshape(N, KVH, 2, 8, half)
    right = recv_ref[:, SEL + 64 :, :].astype(F32).reshape(N, KVH, 2, 8, half)
    causal = lax.broadcasted_iota(jnp.int32, (half, half), 0) >= lax.broadcasted_iota(jnp.int32, (half, half), 1)

    def mix(scores, values):
        top = jnp.max(scores, axis=1, keepdims=True)
        weights = jnp.exp((scores - top) * (HS**-0.5))
        total = jnp.sum(weights, axis=1, keepdims=True)
        product = lax.dot_general(weights.astype(BF), values, NT, preferred_element_type=F32)
        return (product / total).astype(BF)

    for g in range(KVH):
        k_l, v_l = [left[:, g, i].reshape(HS, half).astype(BF) for i in range(2)]
        k_r, v_r = [right[:, g, i].reshape(HS, half).astype(BF) for i in range(2)]
        values = jnp.concatenate([v_l, v_r], axis=1)
        for h in range(g * HQ // KVH, (g + 1) * HQ // KVH):
            here = slice(h * HS, (h + 1) * HS)
            scores = jnp.dot(recv_ref[h, :SEL, :], k_l, preferred_element_type=F32)
            tail = jnp.dot(recv_ref[h, half:SEL, :], k_r, preferred_element_type=F32)
            upper = jnp.where(causal, scores[:half], -1e30)
            lower = jnp.concatenate([scores[half:], jnp.where(causal, tail, -1e30)], axis=1)
            mixed_ref[:half, here] = mix(upper, v_l)
            mixed_ref[half:, here] = mix(lower, values)
    for load in loads:
        load.wait()
    update = jnp.zeros((SEL, SL), F32)
    for h in range(HQ):
        rows = [
            jnp.concatenate(
                [wout_ref[pl.ds(((2 * b + s) * N + h) * PIECE, PIECE), :] for s in range(2)], axis=1
            )
            for b in range(HS // PIECE)
        ]
        update += jnp.dot(
            mixed_ref[:, h * HS : (h + 1) * HS], jnp.concatenate(rows, axis=0), preferred_element_type=F32
        )
    sel_row = sel_ref[...]
    owner = sel_row >> 7
    first = jnp.sum(
        jnp.where(column(sel_row) < owner * TOK, 1.0, 0.0), axis=0, keepdims=True
    ).astype(jnp.int32)
    place = owner * CAP + lax.broadcasted_iota(jnp.int32, (1, SEL), 1) - first
    put = one_hot(lax.broadcasted_iota(jnp.int32, (N * CAP, SEL), 0) == place)
    sent = jnp.dot(put, update.astype(BF), preferred_element_type=F32).astype(BF)
    out_ref[...] = sent.reshape(N, CAP, SL)


def finish_kernel(sel_ref, tok_ref, router_ref, recv_ref, out_ref):
    by_slot, by_token = slots(sel_ref[...], lax.axis_index("ctx"))
    put = lax.dot_general(by_token, by_slot, NT, preferred_element_type=F32).astype(BF)
    live = jnp.sum(by_token.astype(F32), axis=1, keepdims=True) > 0.5
    router = router_ref[...].reshape(1, D).astype(F32)
    logit = jnp.sum(tok_ref[...].astype(F32) * router, axis=1, keepdims=True)
    gate = 1.0 / (1.0 + jnp.exp(-logit))
    for c in range(N):
        part = slice(c * SL, (c + 1) * SL)
        placed = jnp.dot(put, recv_ref[c], preferred_element_type=F32)
        old = tok_ref[:, part]
        fresh = (old.astype(F32) + gate * placed).astype(BF)
        out_ref[:, part] = jnp.where(live, fresh, old)


def call(kernel, name, shapes, in_hbm, flops, moved, scratch=()):
    return pl.pallas_call(
        kernel,
        out_shape=shapes,
        in_specs=[pl.BlockSpec(memory_space=pl.ANY if hbm else VMEM) for hbm in in_hbm],
        out_specs=jax.tree.map(lambda _: pl.BlockSpec(memory_space=VMEM), shapes),
        scratch_shapes=scratch,
        compiler_params=pltpu.CompilerParams(vmem_limit_bytes=40 * 1024 * 1024),
        cost_estimate=pl.CostEstimate(flops=flops, bytes_accessed=moved, transcendentals=0),
        name=name,
    )


def on_device(tokens, selected, norm_gain, router, w_query, w_key, w_value, w_out):
    me = lax.axis_index("ctx")
    shape = jax.ShapeDtypeStruct
    sel = selected.reshape(1, SEL)
    lane = jnp.arange(HS)
    position = selected.astype(F32)[:, None]

    def turn(component, used):
        pair = (component // 2).astype(F32)
        inverse = jnp.exp(-(2.0 * pair / HS) * jnp.log(10000.0))
        angle = position * jnp.where(used, inverse, 0.0)[None, :]
        return jnp.cos(angle), jnp.sin(angle) * jnp.where(component % 2 == 0, -1.0, 1.0)[None, :]

    q_cos, q_sin = turn(lane, lane < HS)
    k_cos, k_sin = turn(me * 8 + lane // 4, lane < 32)
    send = call(
        pack_kernel, "pack", shape((N, 2 * CAP + PIECE, 128), BF), (0, 1, 0, 1), 2 * CAP * TOK * D, 2 << 20,
        [VMEM((TOK, D), BF), VMEM((PIECE, D), BF), pltpu.SemaphoreType.DMA((5,))],
    )(sel, tokens, norm_gain, w_out)
    got = lax.all_to_all(send, "ctx", 0, 0, tiled=True)
    copies, piece = call(
        compact_kernel, "compact", (shape((N, SEL, SL), BF), shape((N * PIECE, 128), BF)), (0, 0),
        2 * SEL * 512 * SL, 3 << 20,
    )(sel, got)
    w_slice = lax.all_gather(piece, "z", axis=0, tiled=True)
    rows = lax.all_to_all(copies, "ctx", 0, 0, tiled=True)
    qkv = call(qkv_kernel, "qkv", shape((N, CHUNK, HS), BF), (0,) * 8, 2 * SEL * D * 256, 6 << 20)(
        rows, w_query, w_key.T, w_value.T, q_cos, q_sin, k_cos, k_sin
    )
    heads = lax.all_to_all(qkv, "ctx", 0, 0, tiled=True)
    update = call(
        attend_kernel, "attend", shape((N, CAP, SL), BF), (0, 0, 1), 2 * 16 * 3 * 256 * 256 * 128, 4 << 20,
        [VMEM((NZ * N * PIECE, 128), BF), VMEM((SEL, HQ * HS), BF), pltpu.SemaphoreType.DMA((4,))],
    )(sel, heads, w_slice)
    back = lax.all_to_all(update, "ctx", 0, 0, tiled=True)
    return call(finish_kernel, "finish", shape((TOK, D), BF), (0,) * 4, 2 * TOK * CAP * D, 4 << 20)(
        sel, tokens, router, back
    )


def solution(mesh):
    split = Mesh(mesh.devices.reshape(NZ, mesh.shape["dp"] // NZ, N), ("z", "core", "ctx"))
    every = ("z", "core", "ctx")
    placed = (
        P(every, None),
        P(("z", "core")),
        P(),
        P(),
        P(None, "ctx"),
        P(None, "ctx"),
        P(None, "ctx"),
        P("ctx", None),
    )
    return jax.shard_map(on_device, mesh=split, in_specs=placed, out_specs=P(every, None), check_vma=False)
```

time: 116 us -> 144 us (1.24)
  the two profiles are of different devices: /device:TPU:480 before, /device:TPU:32 now
where the time goes in v2:
time: 144 us; the launch traced here: 143 us
  waiting for transfers between devices  66.1 us (46%)
  blocking collectives  31.2 us (22%)
  between operations  13.5 us (9%)
  Pallas kernels  11.8 us (8%)
  local copies, waits for them, and re-layouts  10.4 us (7%)
  starting transfers between devices  8.3 us (6%)
  other arithmetic  1.78 us (1%)
    all_gather x1, waiting for transfers between devices, on_device(): w_slice = lax.all_gather(piece, 'z', axis=0, tiled=True)  39.5 us
    all_to_all x1, waiting for transfers between devices, on_device(): rows = lax.all_to_all(copies, 'ctx', 0, 0, tiled=True)  26 us
    all_to_all x1, blocking collectives, on_device(): got = lax.all_to_all(send, 'ctx', 0, 0, tiled=True)  16 us
    all_to_all x1, blocking collectives, on_device(): back = lax.all_to_all(update, 'ctx', 0, 0, tiled=True)  15.2 us
    unnamed x28, local copies, waits for them, and re-layouts  10.4 us
    pallas_call x1, Pallas kernels, on_device(): call(attend_kernel, 'attend', shape((N, CAP, SL), BF), (0, 0, 1), 2 * 16...  6.38 us
    all_to_all x1, starting transfers between devices, on_device(): heads = lax.all_to_all(qkv, 'ctx', 0, 0, tiled=True)  4.41 us
    all_to_all x1, starting transfers between devices, on_device(): rows = lax.all_to_all(copies, 'ctx', 0, 0, tiled=True)  3.85 us
  transfers between devices with their start and end apart: 3, of which 2 were waited for; matrix products, arithmetic and copies ran while one was open for 1% of the time, Pallas kernels for 1%

profile of v2, /device:TPU:32, one launch (start us, length us, event | category | flops | bytes accessed | tf_op | source)
XLA Modules:
  0.0 143.0 jit_solution(1220508225782597646)
XLA Ops:
  6.5 1.2 copy-done.1
  7.8 1.2 copy-done.4
  9.0 0.7 copy-done.9
  9.7 0.7 copy-done.11
  10.4 0.9 pack.1
  11.3 16.0 %all_to_all.20.recv_ref = bf16[16,80,128]{2,1,0:T(8,128)(2,1)S(1)} all-to-all(bf16[16,80,128]{2,1,0:T(8,128)(2,1)S(1)} %pack.1), channel_id=1, replica_groups=mesh['z'=16,'core'=2,'ctx'=16] {'ctx'}, dimensions={0} | all-to-all | bytes 655360 | tf_op jit(solution)/shard_map/all_to_all | solution.py:225
  27.3 0.0 copy-done.10
  27.3 1.0 compact.1
  28.4 1.3 copy-done.3
  29.7 3.8 %all-to-all-start.1 = ((bf16[16,256,256]{2,1,0:T(8,128)(2,1)}), bf16[16,256,256]{2,1,0:T(8,128)(2,1)S(1)}, u32[]{:S(2)}, u32[]{:S(2)}) async-start(bf16[16,256,256]{2,1,0:T(8,128)(2,1)} %copy-done.3), calls=%async_computation.1 | async-start | bytes 4194304 | tf_op jit(solution)/shard_map/all_to_all | solution.py:231
  33.6 0.0 all-gather.2.cloned.1.call-start
  33.6 0.7 all-gather.2.cloned.1.call-update
  34.3 1.7 %fusion.1 = (f32[256,128]{1,0:T(8,128)S(1)}, f32[256,128]{1,0:T(8,128)S(1)}, f32[256,128]{1,0:T(8,128)S(1)}, f32[256,128]{1,0:T(8,128)}) fusion(f32[128]{0:T(128)S(1)} %get-tuple-element.15, f32[128]{0:T(128)S(1)} %get-tuple-element.16, f32[256]{0:T(256)S(1)} %convert_element_type.17, f32[128]{0:T(128)S(1)} %get-tuple-element.18, f32[128]{0:T(128)S(1)} %get-tuple-element.17), kind=kLoop, calls=%fused_computation.5 | loop fusion | flops 131072 | bytes 527360 | tf_op jit(solution)/shard_map/mul | solution.py:217
  36.1 26.0 %all-to-all-done.1.x_ref = bf16[16,256,256]{2,1,0:T(8,128)(2,1)S(1)} async-done(((bf16[16,256,256]{2,1,0:T(8,128)(2,1)}), bf16[16,256,256]{2,1,0:T(8,128)(2,1)S(1)}, u32[]{:S(2)}, u32[]{:S(2)}) %all-to-all-start.1) | async-done | bytes 2097184 | tf_op jit(solution)/shard_map/all_to_all | solution.py:231
  62.1 0.0 copy-done.5
  62.1 0.9 copy-done.6
  63.0 0.9 copy-done.7
  63.9 0.9 copy-done.8
  64.9 1.6 %qkv.1 = bf16[16,384,128]{2,1,0:T(8,128)(2,1)S(1)} custom-call(bf16[16,256,256]{2,1,0:T(8,128)(2,1)S(1)} %all-to-all-done.1.x_ref, bf16[4096,128]{1,0:T(8,128)(2,1)S(1)} %copy-done.5, bf16[32,4096]{1,0:T(8,128)(2,1)S(1)} %bitcast.3, bf16[32,4096]{1,0:T(8,128)(2,1)S(1)} %bitcast.4, f32[256,128]{1,0:T(8,128)S(1)} %get-tuple-element.13.qcos_ref, ...), custom_call_target="tpu_custom_call" | custom-call | flops 536870912 | bytes 6291456 | tf_op jit(solution)/shard_map/qkv/pallas_call | solution.py:232
  66.5 0.0 copy-start
  66.5 1.1 copy-done
  67.7 4.4 %all-to-all-start.2 = ((bf16[16,384,128]{2,1,0:T(8,128)(2,1)}), bf16[16,384,128]{2,1,0:T(8,128)(2,1)}, u32[]{:S(2)}, u32[]{:S(2)}) async-start(bf16[16,384,128]{2,1,0:T(8,128)(2,1)} %copy-done), calls=%async_computation.2 | async-start | bytes 3145728 | tf_op jit(solution)/shard_map/all_to_all | solution.py:235
  72.1 0.0 copy-start.2
  72.1 0.0 copy-start.12
  72.1 39.5 %all-gather.2.cloned.1.call-done.wout_hbm = bf16[4096,128]{1,0:T(8,128)(2,1)} async-done(((bf16[256,128]{1,0:T(8,128)(2,1)}), bf16[4096,128]{1,0:T(8,128)(2,1)}) %all-gather.2.cloned.1.call-update) | async-done | bytes 1048592 | tf_op jit(solution)/shard_map/all_gather | solution.py:230
  111.5 0.0 all-to-all-done.2.recv_ref
  111.6 1.2 copy-done.13
  112.8 6.4 %attend.1 = bf16[16,32,256]{2,1,0:T(8,128)(2,1)S(1)} custom-call(s32[1,256]{1,0:T(1,128)S(1)} %bitcast.7, bf16[16,384,128]{2,1,0:T(8,128)(2,1)} %all-to-all-done.2.recv_ref, bf16[4096,128]{1,0:T(8,128)(2,1)S(1)} %copy-done.13), custom_call_target="tpu_custom_call" | custom-call | flops 805306368 | bytes 4194304 | tf_op jit(solution)/shard_map/attend/pallas_call | solution.py:236
  119.2 15.2 %all_to_all.21.recv_ref = bf16[16,32,256]{2,1,0:T(8,128)(2,1)S(1)} all-to-all(bf16[16,32,256]{2,1,0:T(8,128)(2,1)S(1)} %attend.1), channel_id=1, replica_groups=mesh['z'=16,'core'=2,'ctx'=16] {'ctx'}, dimensions={0} | all-to-all | bytes 524288 | tf_op jit(solution)/shard_map/all_to_all | solution.py:240
  134.3 0.0 copy-done.2
  134.3 0.0 copy-done.12
  134.3 1.8 %finish.1 = bf16[128,4096]{1,0:T(8,128)(2,1)} custom-call(s32[1,256]{1,0:T(1,128)S(1)} %bitcast.8, bf16[128,4096]{1,0:T(8,128)(2,1)S(1)} %copy-done.2, bf16[4096]{0:T(1024)(128)(2,1)S(1)} %copy-done.12, bf16[16,32,256]{2,1,0:T(8,128)(2,1)S(1)} %all_to_all.21.recv_ref), custom_call_target="tpu_custom_call" | custom-call | flops 33554432 | bytes 4194304 | tf_op jit(solution)/shard_map/finish/pallas_call | solution.py:241
  (14 shorter events, 0.0 us)
Async XLA Ops:
  6.5 20.8 %copy-start.10 = (s32[256]{0:T(256)S(1)}, s32[256]{0:T(256)}, u32[]{:S(2)}) copy-start(s32[256]{0:T(256)} %param.9) | copy-start | bytes 3076
  6.5 1.2 copy-start.1
  7.8 1.2 copy-start.4
  9.0 0.7 copy-start.9
  9.7 0.7 copy-start.11
  28.4 1.3 copy-start.3
  29.7 32.4 %copy-start.5 = (bf16[4096,128]{1,0:T(8,128)(2,1)S(1)}, bf16[4096,128]{1,0:T(8,128)(2,1)}, u32[]{:S(2)}) copy-start(bf16[4096,128]{1,0:T(8,128)(2,1)} %wq_ref.1) | copy-start | bytes 3145732
  29.7 32.4 %all-to-all-start.1 = ((bf16[16,256,256]{2,1,0:T(8,128)(2,1)}), bf16[16,256,256]{2,1,0:T(8,128)(2,1)S(1)}, u32[]{:S(2)}, u32[]{:S(2)}) async-start(bf16[16,256,256]{2,1,0:T(8,128)(2,1)} %copy-done.3), calls=%async_computation.1 | async-start | bytes 4194304 | tf_op jit(solution)/shard_map/all_to_all | solution.py:231
  33.6 78.0 %all-gather.2.cloned.1.call-start = ((), (), s32[]{:S(2)}) async-start(), calls=%async_computation.4 | async-start | bytes 1114112 | tf_op jit(solution)/shard_map/all_gather | solution.py:230
  62.1 0.9 copy-start.6
  63.0 0.9 copy-start.7
  63.9 0.9 copy-start.8
  66.5 1.2 copy-start
  67.7 43.9 %all-to-all-start.2 = ((bf16[16,384,128]{2,1,0:T(8,128)(2,1)}), bf16[16,384,128]{2,1,0:T(8,128)(2,1)}, u32[]{:S(2)}, u32[]{:S(2)}) async-start(bf16[16,384,128]{2,1,0:T(8,128)(2,1)} %copy-done), calls=%async_computation.2 | async-start | bytes 3145728 | tf_op jit(solution)/shard_map/all_to_all | solution.py:235
  72.1 62.3 %copy-start.2 = (bf16[128,4096]{1,0:T(8,128)(2,1)S(1)}, bf16[128,4096]{1,0:T(8,128)(2,1)}, u32[]{:S(2)}) copy-start(bf16[128,4096]{1,0:T(8,128)(2,1)} %tok_ref.1) | copy-start | bytes 3145732
  72.1 62.3 %copy-start.12 = (bf16[4096]{0:T(1024)(128)(2,1)S(1)}, bf16[4096]{0:T(1024)(128)(2,1)}, u32[]{:S(2)}) copy-start(bf16[4096]{0:T(1024)(128)(2,1)} %router_ref.1) | copy-start | bytes 24580
  111.6 1.2 copy-start.13
Sparse Core Ops, SparseCore 0:
  36.5 75.0 all-gather.1

commit v3 on v2

--- a/solution.py
+++ b/solution.py
@@ -15,7 +15,7 @@
 SEL = 256
 D = 4096
 SL = D // N
-NZ = 16
+NP = 8
 BF = jnp.bfloat16
 F32 = jnp.float32
 NT = (((1,), (1,)), ((), ()))
@@ -46,7 +46,7 @@
 
 
 def pack_kernel(sel_ref, tok_hbm, gain_ref, wout_hbm, send_ref, tok_ref, wout_ref, sems):
-    z, me = lax.axis_index("z"), lax.axis_index("ctx")
+    part, me = lax.axis_index(("z", "core")), lax.axis_index("ctx")
     parts = 4
     height = TOK // parts
     loads = [
@@ -57,7 +57,7 @@
     ]
     loads.append(
         pltpu.make_async_copy(
-            wout_hbm.at[pl.ds(pl.multiple_of((z // 2) * PIECE, PIECE), PIECE)], wout_ref, sems.at[parts]
+            wout_hbm.at[pl.ds(pl.multiple_of(part * PIECE, PIECE), PIECE)], wout_ref, sems.at[parts]
         )
     )
     for load in loads:
@@ -69,13 +69,11 @@
     raw = jnp.dot(pick, tok_ref[...], preferred_element_type=F32)
     scale = lax.rsqrt(jnp.mean(raw * raw, axis=1, keepdims=True) + 1e-05)
     normed = (raw * scale * gain_ref[...].reshape(1, D).astype(F32)).astype(BF)
-    right = z % 2 == 1
     for c in range(N):
-        send_ref[c, :CAP, :] = normed[:, c * SL : c * SL + 128]
-        send_ref[c, CAP : 2 * CAP, :] = normed[:, c * SL + 128 : (c + 1) * SL]
-        send_ref[c, 2 * CAP :, :] = jnp.where(
-            right, wout_ref[:, c * SL + 128 : (c + 1) * SL], wout_ref[:, c * SL : c * SL + 128]
-        )
+        for i in range(2):
+            part = slice(c * SL + i * 128, c * SL + (i + 1) * 128)
+            send_ref[c, i * CAP : (i + 1) * CAP, :] = normed[:, part]
+            send_ref[c, 2 * CAP + i * PIECE : 2 * CAP + (i + 1) * PIECE, :] = wout_ref[:, part]
 
 
 def compact_kernel(sel_ref, recv_ref, out_ref, piece_ref):
@@ -89,7 +87,7 @@
     dense = jnp.concatenate([left, right], axis=1).astype(BF)
     for d in range(N):
         out_ref[d] = dense
-        piece_ref[d * PIECE : (d + 1) * PIECE, :] = recv_ref[d, 2 * CAP :, :]
+        piece_ref[d * 2 * PIECE : (d + 1) * 2 * PIECE, :] = recv_ref[d, 2 * CAP :, :]
 
 
 def qkv_kernel(x_ref, wq_ref, wk_ref, wv_ref, qcos_ref, qsin_ref, kcos_ref, ksin_ref, out_ref):
@@ -118,7 +116,7 @@
 
 def attend_kernel(sel_ref, recv_ref, wout_hbm, out_ref, wout_ref, mixed_ref, sems):
     parts = 4
-    height = NZ * N * PIECE // parts
+    height = NP * N * 2 * PIECE // parts
     loads = [
         pltpu.make_async_copy(
             wout_hbm.at[pl.ds(i * height, height)], wout_ref.at[pl.ds(i * height, height)], sems.at[i]
@@ -127,39 +125,30 @@
     ]
     for load in loads:
         load.start()
-    half = SEL // 2
-    left = recv_ref[:, SEL : SEL + 64, :].astype(F32).reshape(N, KVH, 2, 8, half)
-    right = recv_ref[:, SEL + 64 :, :].astype(F32).reshape(N, KVH, 2, 8, half)
-    causal = lax.broadcasted_iota(jnp.int32, (half, half), 0) >= lax.broadcasted_iota(jnp.int32, (half, half), 1)
-
-    def mix(scores, values):
-        top = jnp.max(scores, axis=1, keepdims=True)
-        weights = jnp.exp((scores - top) * (HS**-0.5))
-        total = jnp.sum(weights, axis=1, keepdims=True)
-        product = lax.dot_general(weights.astype(BF), values, NT, preferred_element_type=F32)
-        return (product / total).astype(BF)
-
+    left = recv_ref[:, SEL : SEL + 64, :].astype(F32).reshape(N, KVH, 2, 8, 128)
+    right = recv_ref[:, SEL + 64 :, :].astype(F32).reshape(N, KVH, 2, 8, 128)
+    causal = lax.broadcasted_iota(jnp.int32, (SEL, SEL), 0) >= lax.broadcasted_iota(jnp.int32, (SEL, SEL), 1)
     for g in range(KVH):
-        k_l, v_l = [left[:, g, i].reshape(HS, half).astype(BF) for i in range(2)]
-        k_r, v_r = [right[:, g, i].reshape(HS, half).astype(BF) for i in range(2)]
-        values = jnp.concatenate([v_l, v_r], axis=1)
+        keys, values = [
+            jnp.concatenate([half[:, g, i].reshape(HS, 128) for half in (left, right)], axis=1).astype(BF)
+            for i in range(2)
+        ]
         for h in range(g * HQ // KVH, (g + 1) * HQ // KVH):
-            here = slice(h * HS, (h + 1) * HS)
-            scores = jnp.dot(recv_ref[h, :SEL, :], k_l, preferred_element_type=F32)
-            tail = jnp.dot(recv_ref[h, half:SEL, :], k_r, preferred_element_type=F32)
-            upper = jnp.where(causal, scores[:half], -1e30)
-            lower = jnp.concatenate([scores[half:], jnp.where(causal, tail, -1e30)], axis=1)
-            mixed_ref[:half, here] = mix(upper, v_l)
-            mixed_ref[half:, here] = mix(lower, values)
+            scores = jnp.dot(recv_ref[h, :SEL, :], keys, preferred_element_type=F32) * (HS**-0.5)
+            scores = jnp.where(causal, scores, -1e30)
+            weights = jnp.exp(scores - jnp.max(scores, axis=1, keepdims=True))
+            probs = (weights / jnp.sum(weights, axis=1, keepdims=True)).astype(BF)
+            mixed = lax.dot_general(probs, values, NT, preferred_element_type=F32)
+            mixed_ref[:, h * HS : (h + 1) * HS] = mixed.astype(BF)
     for load in loads:
         load.wait()
     update = jnp.zeros((SEL, SL), F32)
     for h in range(HQ):
         rows = [
             jnp.concatenate(
-                [wout_ref[pl.ds(((2 * b + s) * N + h) * PIECE, PIECE), :] for s in range(2)], axis=1
+                [wout_ref[pl.ds(((m * N + h) * 2 + i) * PIECE, PIECE), :] for i in range(2)], axis=1
             )
-            for b in range(HS // PIECE)
+            for m in range(NP)
         ]
         update += jnp.dot(
             mixed_ref[:, h * HS : (h + 1) * HS], jnp.concatenate(rows, axis=0), preferred_element_type=F32
@@ -219,15 +208,15 @@
     q_cos, q_sin = turn(lane, lane < HS)
     k_cos, k_sin = turn(me * 8 + lane // 4, lane < 32)
     send = call(
-        pack_kernel, "pack", shape((N, 2 * CAP + PIECE, 128), BF), (0, 1, 0, 1), 2 * CAP * TOK * D, 2 << 20,
+        pack_kernel, "pack", shape((N, 2 * CAP + 2 * PIECE, 128), BF), (0, 1, 0, 1), 2 * CAP * TOK * D, 2 << 20,
         [VMEM((TOK, D), BF), VMEM((PIECE, D), BF), pltpu.SemaphoreType.DMA((5,))],
     )(sel, tokens, norm_gain, w_out)
     got = lax.all_to_all(send, "ctx", 0, 0, tiled=True)
     copies, piece = call(
-        compact_kernel, "compact", (shape((N, SEL, SL), BF), shape((N * PIECE, 128), BF)), (0, 0),
+        compact_kernel, "compact", (shape((N, SEL, SL), BF), shape((N * 2 * PIECE, 128), BF)), (0, 0),
         2 * SEL * 512 * SL, 3 << 20,
     )(sel, got)
-    w_slice = lax.all_gather(piece, "z", axis=0, tiled=True)
+    w_slice = lax.all_gather(piece, ("z", "core"), axis=0, tiled=True)
     rows = lax.all_to_all(copies, "ctx", 0, 0, tiled=True)
     qkv = call(qkv_kernel, "qkv", shape((N, CHUNK, HS), BF), (0,) * 8, 2 * SEL * D * 256, 6 << 20)(
         rows, w_query, w_key.T, w_value.T, q_cos, q_sin, k_cos, k_sin
@@ -235,7 +224,7 @@
     heads = lax.all_to_all(qkv, "ctx", 0, 0, tiled=True)
     update = call(
         attend_kernel, "attend", shape((N, CAP, SL), BF), (0, 0, 1), 2 * 16 * 3 * 256 * 256 * 128, 4 << 20,
-        [VMEM((NZ * N * PIECE, 128), BF), VMEM((SEL, HQ * HS), BF), pltpu.SemaphoreType.DMA((4,))],
+        [VMEM((NP * N * 2 * PIECE, 128), BF), VMEM((SEL, HQ * HS), BF), pltpu.SemaphoreType.DMA((4,))],
     )(sel, heads, w_slice)
     back = lax.all_to_all(update, "ctx", 0, 0, tiled=True)
     return call(finish_kernel, "finish", shape((TOK, D), BF), (0,) * 4, 2 * TOK * CAP * D, 4 << 20)(
@@ -244,11 +233,11 @@
 
 
 def solution(mesh):
-    split = Mesh(mesh.devices.reshape(NZ, mesh.shape["dp"] // NZ, N), ("z", "core", "ctx"))
-    every = ("z", "core", "ctx")
+    split = Mesh(mesh.devices.reshape(-1, 4, 2, N), ("block", "z", "core", "ctx"))
+    every = ("block", "z", "core", "ctx")
     placed = (
         P(every, None),
-        P(("z", "core")),
+        P(("block", "z", "core")),
         P(),
         P(),
         P(None, "ctx"),

time: 144 us -> 123 us (0.85)
  the two profiles are of different devices: /device:TPU:32 before, /device:TPU:480 now
where the time goes in v3:
time: 123 us; the launch traced here: 122 us
  waiting for transfers between devices  47 us (38%)
  blocking collectives  28.6 us (23%)
  between operations  13.5 us (11%)
  Pallas kernels  12.4 us (10%)
  local copies, waits for them, and re-layouts  10.4 us (8%)
  starting transfers between devices  8.3 us (7%)
  other arithmetic  1.78 us (1%)
    all_to_all x1, waiting for transfers between devices, on_device(): rows = lax.all_to_all(copies, 'ctx', 0, 0, tiled=True)  26 us
    all_to_all x1, waiting for transfers between devices, on_device(): heads = lax.all_to_all(qkv, 'ctx', 0, 0, tiled=True)  17.7 us
    all_to_all x1, blocking collectives, on_device(): got = lax.all_to_all(send, 'ctx', 0, 0, tiled=True)  16.7 us
    all_to_all x1, blocking collectives, on_device(): back = lax.all_to_all(update, 'ctx', 0, 0, tiled=True)  11.9 us
    unnamed x28, local copies, waits for them, and re-layouts  10.4 us
    pallas_call x1, Pallas kernels, on_device(): call(attend_kernel, 'attend', shape((N, CAP, SL), BF), (0, 0, 1), 2 * 16...  6.99 us
    all_to_all x1, starting transfers between devices, on_device(): heads = lax.all_to_all(qkv, 'ctx', 0, 0, tiled=True)  4.41 us
    all_to_all x1, starting transfers between devices, on_device(): rows = lax.all_to_all(copies, 'ctx', 0, 0, tiled=True)  3.86 us
  transfers between devices with their start and end apart: 3, of which 3 were waited for; matrix products, arithmetic and copies ran while one was open for 1% of the time, Pallas kernels for 1%

profile of v3, /device:TPU:480, one launch (start us, length us, event | category | flops | bytes accessed | tf_op | source)
XLA Modules:
  0.0 121.9 jit_solution(5302510570536755430)
XLA Ops:
  6.5 1.2 %copy-done.1 = bf16[128,4096]{1,0:T(8,128)(2,1)S(1)} copy-done((bf16[128,4096]{1,0:T(8,128)(2,1)S(1)}, bf16[128,4096]{1,0:T(8,128)(2,1)}, u32[]{:S(2)}) %copy-start.1) | copy-done | bytes 1048600
  7.8 1.2 %copy-done.4 = bf16[128,4096]{1,0:T(8,128)(2,1)S(1)} copy-done((bf16[128,4096]{1,0:T(8,128)(2,1)S(1)}, bf16[128,4096]{1,0:T(8,128)(2,1)}, u32[]{:S(2)}) %copy-start.4) | copy-done | bytes 1048600
  9.0 0.7 copy-done.9
  9.7 0.7 copy-done.11
  10.4 0.9 pack.1
  11.3 16.7 %all_to_all.20.recv_ref = bf16[16,96,128]{2,1,0:T(8,128)(2,1)S(1)} all-to-all(bf16[16,96,128]{2,1,0:T(8,128)(2,1)S(1)} %pack.1), channel_id=1, replica_groups=mesh['block'=4,'z'=4,'core'=2,'ctx'=16] {'ctx'}, dimensions={0} | all-to-all | bytes 786432 | tf_op jit(solution)/shard_map/all_to_all | solution.py:214
  28.0 0.0 copy-done.10
  28.0 1.1 compact.1
  29.1 1.3 %copy-done.3 = bf16[16,256,256]{2,1,0:T(8,128)(2,1)} copy-done((bf16[16,256,256]{2,1,0:T(8,128)(2,1)}, bf16[16,256,256]{2,1,0:T(8,128)(2,1)S(1)}, u32[]{:S(2)}) %copy-start.3) | copy-done | bytes 2097176
  30.4 3.9 %all-to-all-start.1 = ((bf16[16,256,256]{2,1,0:T(8,128)(2,1)}), bf16[16,256,256]{2,1,0:T(8,128)(2,1)S(1)}, u32[]{:S(2)}, u32[]{:S(2)}) async-start(bf16[16,256,256]{2,1,0:T(8,128)(2,1)} %copy-done.3), calls=%async_computation.1 | async-start | bytes 4194304 | tf_op jit(solution)/shard_map/all_to_all | solution.py:220
  34.3 0.0 all-gather.2.cloned.1.call-start
  34.4 0.6 all-gather.2.cloned.1.call-update
  35.0 1.7 %fusion.1 = (f32[256,128]{1,0:T(8,128)S(1)}, f32[256,128]{1,0:T(8,128)S(1)}, f32[256,128]{1,0:T(8,128)S(1)}, f32[256,128]{1,0:T(8,128)}) fusion(f32[128]{0:T(128)S(1)} %get-tuple-element.15, f32[128]{0:T(128)S(1)} %get-tuple-element.16, f32[256]{0:T(256)S(1)} %convert_element_type.17, f32[128]{0:T(128)S(1)} %get-tuple-element.18, f32[128]{0:T(128)S(1)} %get-tuple-element.17), kind=kLoop, calls=%fused_computation.5 | loop fusion | flops 131072 | bytes 527360 | tf_op jit(solution)/shard_map/mul | solution.py:206
  36.8 26.0 %all-to-all-done.1.x_ref = bf16[16,256,256]{2,1,0:T(8,128)(2,1)S(1)} async-done(((bf16[16,256,256]{2,1,0:T(8,128)(2,1)}), bf16[16,256,256]{2,1,0:T(8,128)(2,1)S(1)}, u32[]{:S(2)}, u32[]{:S(2)}) %all-to-all-start.1) | async-done | bytes 2097184 | tf_op jit(solution)/shard_map/all_to_all | solution.py:220
  62.8 0.0 copy-done.5
  62.8 0.9 copy-done.6
  63.7 0.9 copy-done.7
  64.7 0.9 copy-done.8
  65.6 1.6 %qkv.1 = bf16[16,384,128]{2,1,0:T(8,128)(2,1)S(1)} custom-call(bf16[16,256,256]{2,1,0:T(8,128)(2,1)S(1)} %all-to-all-done.1.x_ref, bf16[4096,128]{1,0:T(8,128)(2,1)S(1)} %copy-done.5, bf16[32,4096]{1,0:T(8,128)(2,1)S(1)} %bitcast.3, bf16[32,4096]{1,0:T(8,128)(2,1)S(1)} %bitcast.4, f32[256,128]{1,0:T(8,128)S(1)} %get-tuple-element.13.qcos_ref, ...), custom_call_target="tpu_custom_call" | custom-call | flops 536870912 | bytes 6291456 | tf_op jit(solution)/shard_map/qkv/pallas_call | solution.py:221
  67.2 0.0 copy-start
  67.3 1.1 copy-done
  68.4 4.4 %all-to-all-start.2 = ((bf16[16,384,128]{2,1,0:T(8,128)(2,1)}), bf16[16,384,128]{2,1,0:T(8,128)(2,1)}, u32[]{:S(2)}, u32[]{:S(2)}) async-start(bf16[16,384,128]{2,1,0:T(8,128)(2,1)} %copy-done), calls=%async_computation.2 | async-start | bytes 3145728 | tf_op jit(solution)/shard_map/all_to_all | solution.py:224
  72.8 0.0 copy-start.2
  72.8 0.0 copy-start.12
  72.8 2.6 %all-gather.2.cloned.1.call-done.wout_hbm = bf16[4096,128]{1,0:T(8,128)(2,1)} async-done(((bf16[512,128]{1,0:T(8,128)(2,1)}), bf16[4096,128]{1,0:T(8,128)(2,1)}) %all-gather.2.cloned.1.call-update) | async-done | bytes 1048592 | tf_op jit(solution)/shard_map/all_gather | solution.py:219
  75.5 17.7 %all-to-all-done.2.recv_ref = bf16[16,384,128]{2,1,0:T(8,128)(2,1)} async-done(((bf16[16,384,128]{2,1,0:T(8,128)(2,1)}), bf16[16,384,128]{2,1,0:T(8,128)(2,1)}, u32[]{:S(2)}, u32[]{:S(2)}) %all-to-all-start.2) | async-done | bytes 1572896 | tf_op jit(solution)/shard_map/all_to_all | solution.py:224
  93.2 1.2 %copy-done.13 = bf16[4096,128]{1,0:T(8,128)(2,1)S(1)} copy-done((bf16[4096,128]{1,0:T(8,128)(2,1)S(1)}, bf16[4096,128]{1,0:T(8,128)(2,1)}, u32[]{:S(2)}) %copy-start.13) | copy-done | bytes 1048600
  94.4 7.0 %attend.1 = bf16[16,32,256]{2,1,0:T(8,128)(2,1)S(1)} custom-call(s32[1,256]{1,0:T(1,128)S(1)} %bitcast.7, bf16[16,384,128]{2,1,0:T(8,128)(2,1)} %all-to-all-done.2.recv_ref, bf16[4096,128]{1,0:T(8,128)(2,1)S(1)} %copy-done.13), custom_call_target="tpu_custom_call" | custom-call | flops 805306368 | bytes 4194304 | tf_op jit(solution)/shard_map/attend/pallas_call | solution.py:225
  101.4 11.9 %all_to_all.21.recv_ref = bf16[16,32,256]{2,1,0:T(8,128)(2,1)S(1)} all-to-all(bf16[16,32,256]{2,1,0:T(8,128)(2,1)S(1)} %attend.1), channel_id=1, replica_groups=mesh['block'=4,'z'=4,'core'=2,'ctx'=16] {'ctx'}, dimensions={0} | all-to-all | bytes 524288 | tf_op jit(solution)/shard_map/all_to_all | solution.py:229
  113.3 0.0 copy-done.2
  113.3 0.0 copy-done.12
  113.3 1.8 %finish.1 = bf16[128,4096]{1,0:T(8,128)(2,1)} custom-call(s32[1,256]{1,0:T(1,128)S(1)} %bitcast.8, bf16[128,4096]{1,0:T(8,128)(2,1)S(1)} %copy-done.2, bf16[4096]{0:T(1024)(128)(2,1)S(1)} %copy-done.12, bf16[16,32,256]{2,1,0:T(8,128)(2,1)S(1)} %all_to_all.21.recv_ref), custom_call_target="tpu_custom_call" | custom-call | flops 33554432 | bytes 4194304 | tf_op jit(solution)/shard_map/finish/pallas_call | solution.py:230
  (14 shorter events, 0.0 us)
Async XLA Ops:
  6.5 21.5 %copy-start.10 = (s32[256]{0:T(256)S(1)}, s32[256]{0:T(256)}, u32[]{:S(2)}) copy-start(s32[256]{0:T(256)} %param.9) | copy-start | bytes 3076
  6.5 1.2 %copy-start.1 = (bf16[128,4096]{1,0:T(8,128)(2,1)S(1)}, bf16[128,4096]{1,0:T(8,128)(2,1)}, u32[]{:S(2)}) copy-start(bf16[128,4096]{1,0:T(8,128)(2,1)} %tok_ref.1) | copy-start | bytes 3145732
  7.8 1.2 %copy-start.4 = (bf16[128,4096]{1,0:T(8,128)(2,1)S(1)}, bf16[128,4096]{1,0:T(8,128)(2,1)}, u32[]{:S(2)}) copy-start(bf16[128,4096]{1,0:T(8,128)(2,1)} %wout_hbm.1) | copy-start | bytes 3145732
  9.0 0.7 copy-start.9
  9.7 0.7 copy-start.11
  29.1 1.3 %copy-start.3 = (bf16[16,256,256]{2,1,0:T(8,128)(2,1)}, bf16[16,256,256]{2,1,0:T(8,128)(2,1)S(1)}, u32[]{:S(2)}) copy-start(bf16[16,256,256]{2,1,0:T(8,128)(2,1)S(1)} %get-tuple-element.7) | copy-start | bytes 6291460
  30.4 32.4 %copy-start.5 = (bf16[4096,128]{1,0:T(8,128)(2,1)S(1)}, bf16[4096,128]{1,0:T(8,128)(2,1)}, u32[]{:S(2)}) copy-start(bf16[4096,128]{1,0:T(8,128)(2,1)} %wq_ref.1) | copy-start | bytes 3145732
  30.4 32.4 %all-to-all-start.1 = ((bf16[16,256,256]{2,1,0:T(8,128)(2,1)}), bf16[16,256,256]{2,1,0:T(8,128)(2,1)S(1)}, u32[]{:S(2)}, u32[]{:S(2)}) async-start(bf16[16,256,256]{2,1,0:T(8,128)(2,1)} %copy-done.3), calls=%async_computation.1 | async-start | bytes 4194304 | tf_op jit(solution)/shard_map/all_to_all | solution.py:220
  34.3 41.2 %all-gather.2.cloned.1.call-start = ((), (), s32[]{:S(2)}) async-start(), calls=%async_computation.4 | async-start | bytes 1179648 | tf_op jit(solution)/shard_map/all_gather | solution.py:219
  62.8 0.9 copy-start.6
  63.7 0.9 copy-start.7
  64.7 0.9 copy-start.8
  67.2 1.2 copy-start
  68.4 24.8 %all-to-all-start.2 = ((bf16[16,384,128]{2,1,0:T(8,128)(2,1)}), bf16[16,384,128]{2,1,0:T(8,128)(2,1)}, u32[]{:S(2)}, u32[]{:S(2)}) async-start(bf16[16,384,128]{2,1,0:T(8,128)(2,1)} %copy-done), calls=%async_computation.2 | async-start | bytes 3145728 | tf_op jit(solution)/shard_map/all_to_all | solution.py:224
  72.8 40.5 %copy-start.2 = (bf16[128,4096]{1,0:T(8,128)(2,1)S(1)}, bf16[128,4096]{1,0:T(8,128)(2,1)}, u32[]{:S(2)}) copy-start(bf16[128,4096]{1,0:T(8,128)(2,1)} %tok_ref.1) | copy-start | bytes 3145732
  72.8 40.5 %copy-start.12 = (bf16[4096]{0:T(1024)(128)(2,1)S(1)}, bf16[4096]{0:T(1024)(128)(2,1)}, u32[]{:S(2)}) copy-start(bf16[4096]{0:T(1024)(128)(2,1)} %router_ref.1) | copy-start | bytes 24580
  93.2 1.2 %copy-start.13 = (bf16[4096,128]{1,0:T(8,128)(2,1)S(1)}, bf16[4096,128]{1,0:T(8,128)(2,1)}, u32[]{:S(2)}) copy-start(bf16[4096,128]{1,0:T(8,128)(2,1)} %all-gather.2.cloned.1.call-done.wout_hbm) | copy-start | bytes 3145732
Sparse Core Ops, SparseCore 0:
  37.2 38.2 all-gather.1

commit v4 on v3

v4 whole, which is shorter than its diff:
```python
import jax
import jax.numpy as jnp
from jax import lax
from jax.experimental import pallas as pl
from jax.experimental.pallas import tpu as pltpu
from jax.sharding import Mesh
from jax.sharding import PartitionSpec as P

HS = 128
HQ = 16
KVH = 4
CAP = 32
N = 16
G = 4
TOK = 128
SEL = 256
D = 4096
Q = D // G
H = Q // 2
BF = jnp.bfloat16
F32 = jnp.float32
NT = (((1,), (1,)), ((), ()))
CHUNK = SEL + SEL // 2
VMEM = pltpu.VMEM


def one_hot(mask):
    return jnp.where(mask, 1.0, 0.0).astype(BF)


def iota(shape, axis):
    return lax.broadcasted_iota(jnp.int32, shape, axis)


def slots(sel, me):
    base = me * TOK
    first = jnp.sum(jnp.where(sel < base, 1.0, 0.0), axis=1, keepdims=True).astype(jnp.int32)
    mine = (sel >= base) & (sel < base + TOK)
    by_slot = one_hot((iota((CAP, SEL), 1) - first == iota((CAP, SEL), 0)) & mine)
    by_token = one_hot(iota((TOK, SEL), 0) + base == sel)
    return by_slot, by_token


def column(row):
    same = iota((SEL, SEL), 0) == iota((SEL, SEL), 1)
    return jnp.sum(jnp.where(same, row.astype(F32), 0.0), axis=1, keepdims=True).astype(jnp.int32)


def pack_kernel(sel_ref, gain_ref, tok_hbm, wq_hbm, wk_hbm, wv_hbm, send_ref, tok_ref, sems):
    me, core = lax.axis_index(("x", "y")), lax.axis_index("core")
    loads = []

    def load(source, target):
        loads.append(pltpu.make_async_copy(source, target, sems.at[len(loads)]))
        loads[-1].start()

    for i in range(4):
        load(tok_hbm.at[pl.ds(i * 32, 32)], tok_ref.at[pl.ds(i * 32, 32)])
    for t in range(G):
        start = pl.multiple_of(t * Q + core * H, H)
        for i in range(4):
            load(wq_hbm.at[pl.ds(start + i * 128, 128)], send_ref.at[t, pl.ds(0, 128), pl.ds(i * 128, 128)])
        load(wk_hbm.at[:, pl.ds(start, H)], send_ref.at[t, pl.ds(128, 32)])
        load(wv_hbm.at[:, pl.ds(start, H)], send_ref.at[t, pl.ds(160, 32)])
    by_slot, by_token = slots(sel_ref[...], me)
    pick = lax.dot_general(by_slot, by_token, NT, preferred_element_type=F32).astype(BF)
    for copy in loads[:4]:
        copy.wait()
    raw = jnp.dot(pick, tok_ref[...], preferred_element_type=F32)
    scale = lax.rsqrt(jnp.mean(raw * raw, axis=1, keepdims=True) + 1e-05)
    normed = (raw * scale * gain_ref[...].reshape(1, D).astype(F32)).astype(BF)
    for t in range(G):
        send_ref[t, 192:224, :] = normed[:, t * Q : t * Q + H]
        send_ref[t, 224:256, :] = normed[:, t * Q + H : (t + 1) * Q]
    for copy in loads[4:]:
        copy.wait()


def spread_kernel(got_ref, wout_hbm, send_ref, sems):
    core = lax.axis_index("core")
    loads = []
    for t in range(G):
        for i in range(2):
            loads.append(
                pltpu.make_async_copy(
                    wout_hbm.at[pl.ds(pl.multiple_of(core * 64, 64), 64), pl.ds(t * Q + i * H, H)],
                    send_ref.at[t, pl.ds(256 + i * 64, 64)],
                    sems.at[len(loads)],
                )
            )
            loads[-1].start()
    for s in range(G):
        rows = got_ref[s, 192:256, :]
        for t in range(G):
            send_ref[t, s * 64 : (s + 1) * 64, :] = rows
    for copy in loads:
        copy.wait()


def project_kernel(sel_ref, rows_ref, own_ref, other_ref, send_ref, wout_ref, x_ref):
    core = lax.axis_index("core")
    sel_row = sel_ref[...]
    owner = column(sel_row) >> 7
    first = jnp.sum(jnp.where(sel_row < owner * TOK, 1.0, 0.0), axis=1, keepdims=True).astype(jnp.int32)
    place = ((owner & 3) * G + (owner >> 2)) * CAP + iota((SEL, 1), 0) - first
    pick = one_hot(iota((SEL, N * CAP), 1) == place)
    for i in range(2):
        padded = jnp.concatenate(
            [rows_ref[s, t * 64 + i * 32 : t * 64 + (i + 1) * 32, :] for s in range(G) for t in range(G)], axis=0
        )
        x_ref[i] = jnp.dot(pick, padded, preferred_element_type=F32).astype(BF)
    q = jnp.zeros((SEL, G * HS), F32)
    kv = jnp.zeros((SEL, G * 64), F32)
    for w_ref, i in ((own_ref, core), (other_ref, 1 - core)):
        w_q = jnp.concatenate(
            [
                jnp.concatenate([w_ref[s, :128, b * 128 : (b + 1) * 128] for b in range(4)], axis=0)
                for s in range(G)
            ],
            axis=1,
        )
        w_kv = jnp.concatenate([w_ref[s, 128:192, :] for s in range(G)], axis=0)
        q += jnp.dot(x_ref[i], w_q, preferred_element_type=F32)
        kv += lax.dot_general(x_ref[i], w_kv, NT, preferred_element_type=F32)
    to, frm = iota((SEL, SEL), 0), iota((SEL, SEL), 1)
    order = one_hot(frm == ((to >> 4) & 3) * 64 + ((to >> 3) & 1) * 32 + (to & 7) * 4 + (to >> 6))
    turned = lax.dot_general(order, kv.astype(BF), NT, preferred_element_type=F32).astype(BF)
    for t in range(G):
        send_ref[t, :SEL, :] = q[:, t * HS : (t + 1) * HS].astype(BF)
        send_ref[t, SEL : SEL + 64, :] = turned[t * 64 : (t + 1) * 64, :128]
        send_ref[t, SEL + 64 :, :] = turned[t * 64 : (t + 1) * 64, 128:]
        wout_ref[t] = rows_ref[t, 256:, :]


def turn_kernel(parts_ref, q_cos_ref, q_sin_ref, k_cos_ref, k_sin_ref, send_ref):
    total = sum(parts_ref[s].astype(F32) for s in range(G))
    q = total[:SEL]
    mate = jnp.where(iota((SEL, HS), 1) % 2 == 0, pltpu.roll(q, HS - 1, 1), pltpu.roll(q, 1, 1))
    q = (q * q_cos_ref[...] + mate * q_sin_ref[...]).astype(BF)
    kv = jnp.concatenate([total[SEL : SEL + 64], total[SEL + 64 :]], axis=1)
    mate = jnp.where(iota((64, SEL), 0) % 2 == 0, pltpu.roll(kv, 63, 0), pltpu.roll(kv, 1, 0))
    kv = (kv * k_cos_ref[...] + mate * k_sin_ref[...]).astype(BF)
    for t in range(G):
        send_ref[t, :SEL, :] = q
        send_ref[t, SEL : SEL + 64, :] = kv[:, :128]
        send_ref[t, SEL + 64 :, :] = kv[:, 128:]


def attend_kernel(sel_ref, heads_ref, own_ref, other_ref, out_ref, mixed_ref):
    core = lax.axis_index("core")
    halves = [
        heads_ref[:, SEL + i * 64 : SEL + (i + 1) * 64, :].astype(F32).reshape(G, G, 2, 8, 128) for i in range(2)
    ]
    keys, values = [
        jnp.concatenate(
            [
                jnp.concatenate([half[y, x, i] for x in range(G) for y in range(G)], axis=0).astype(BF)
                for half in halves
            ],
            axis=1,
        )
        for i in range(2)
    ]
    causal = iota((SEL, SEL), 0) >= iota((SEL, SEL), 1)
    for h in range(G):
        scores = jnp.dot(heads_ref[h, :SEL, :], keys, preferred_element_type=F32) * (HS**-0.5)
        scores = jnp.where(causal, scores, -1e30)
        weights = jnp.exp(scores - jnp.max(scores, axis=1, keepdims=True))
        probs = (weights / jnp.sum(weights, axis=1, keepdims=True)).astype(BF)
        mixed = lax.dot_general(probs, values, NT, preferred_element_type=F32)
        mixed_ref[:, h * HS : (h + 1) * HS] = mixed.astype(BF)
    sel_row = sel_ref[...]
    owner = sel_row >> 7
    first = jnp.sum(
        jnp.where(column(sel_row) < owner * TOK, 1.0, 0.0), axis=0, keepdims=True
    ).astype(jnp.int32)
    place = owner * CAP + iota((1, SEL), 1) - first
    put = one_hot(iota((N * CAP, SEL), 0) == place)
    for i in range(2):
        rows = []
        for h in range(G):
            own, other = own_ref[h, i * 64 : (i + 1) * 64, :], other_ref[h, i * 64 : (i + 1) * 64, :]
            rows += [jnp.where(core == 0, own, other), jnp.where(core == 0, other, own)]
        update = jnp.dot(mixed_ref[...], jnp.concatenate(rows, axis=0), preferred_element_type=F32).astype(BF)
        sent = jnp.dot(put, update, preferred_element_type=F32).astype(BF)
        out_ref[:, :, i * H : (i + 1) * H] = sent.reshape(N, CAP, H)


def finish_kernel(sel_ref, tok_ref, router_ref, parts_ref, out_ref):
    by_slot, by_token = slots(sel_ref[...], lax.axis_index(("x", "y")))
    put = lax.dot_general(by_token, by_slot, NT, preferred_element_type=F32).astype(BF)
    put = jnp.concatenate([put] * G, axis=1)
    live = jnp.sum(by_token.astype(F32), axis=1, keepdims=True) > 0.5
    router = router_ref[...].reshape(1, D).astype(F32)
    logit = jnp.sum(tok_ref[...].astype(F32) * router, axis=1, keepdims=True)
    gate = 1.0 / (1.0 + jnp.exp(-logit))
    for y in range(G):
        terms = jnp.concatenate([parts_ref[x * G + y] for x in range(G)], axis=0)
        placed = jnp.dot(put, terms, preferred_element_type=F32)
        part = slice(y * Q, (y + 1) * Q)
        old = tok_ref[:, part]
        fresh = (old.astype(F32) + gate * placed).astype(BF)
        out_ref[:, part] = jnp.where(live, fresh, old)


def call(kernel, name, shapes, in_hbm, flops, moved, scratch=()):
    return pl.pallas_call(
        kernel,
        out_shape=shapes,
        in_specs=[pl.BlockSpec(memory_space=pl.ANY if hbm else VMEM) for hbm in in_hbm],
        out_specs=jax.tree.map(lambda _: pl.BlockSpec(memory_space=VMEM), shapes),
        scratch_shapes=scratch,
        compiler_params=pltpu.CompilerParams(vmem_limit_bytes=40 * 1024 * 1024),
        cost_estimate=pl.CostEstimate(flops=flops, bytes_accessed=moved, transcendentals=0),
        name=name,
    )


def on_device(tokens, selected, norm_gain, router, w_query, w_key, w_value, w_out):
    y = lax.axis_index("y")
    shape = jax.ShapeDtypeStruct
    dma = pltpu.SemaphoreType.DMA
    sel = selected.reshape(1, SEL)
    position = selected.astype(F32)

    def turn(component, used):
        pair = (component // 2).astype(F32)
        inverse = jnp.exp(-(2.0 * pair / HS) * jnp.log(10000.0))
        return jnp.where(used, inverse, 0.0), jnp.where(component % 2 == 0, -1.0, 1.0)

    lane = jnp.arange(HS)
    inverse, sign = turn(lane, True)
    angle = position[:, None] * inverse[None, :]
    q_cos, q_sin = jnp.cos(angle), jnp.sin(angle) * sign[None, :]
    row = jnp.arange(64)
    inverse, sign = turn(8 * (G * (row // 16) + y) + row % 8, row % 16 < 8)
    angle = inverse[:, None] * position[None, :]
    k_cos, k_sin = jnp.cos(angle), jnp.sin(angle) * sign[:, None]

    def swap(half):
        return lax.ppermute(half, "core", [(0, 1), (1, 0)])

    send = call(
        pack_kernel, "pack", shape((G, 256, H), BF), (0, 0, 1, 1, 1, 1), 2 * CAP * TOK * D, 2 << 20,
        [VMEM((TOK, D), BF), dma((4 + 6 * G,))],
    )(sel, norm_gain, tokens, w_query, w_key.T, w_value.T)
    own = lax.all_to_all(send, "x", 0, 0, tiled=True)
    other = swap(own)
    send = call(
        spread_kernel, "spread", shape((G, 384, H), BF), (0, 1), 1 << 20, 3 << 20, [dma((2 * G,))]
    )(own, w_out)
    rows = lax.all_to_all(send, "y", 0, 0, tiled=True)
    send, w_own = call(
        project_kernel, "project", (shape((G, CHUNK, HS), BF), shape((G, 128, H), BF)), (0,) * 4,
        2 * SEL * Q * 1280, 5 << 20, [VMEM((2, SEL, H), BF)],
    )(sel, rows, own, other)
    w_other = swap(w_own)
    parts = lax.all_to_all(send, "x", 0, 0, tiled=True)
    send = call(turn_kernel, "turn", shape((G, CHUNK, HS), BF), (0,) * 5, SEL * HS * 20, 1 << 20)(
        parts, q_cos, q_sin, k_cos, k_sin
    )
    heads = lax.all_to_all(send, "y", 0, 0, tiled=True)
    send = call(
        attend_kernel, "attend", shape((N, CAP, Q), BF), (0,) * 4, 2 * SEL * 1024 * 1300, 4 << 20,
        [VMEM((SEL, G * HS), BF)],
    )(sel, heads, w_own, w_other)
    parts = lax.all_to_all(send, ("x", "y"), 0, 0, tiled=True)
    return call(finish_kernel, "finish", shape((TOK, D), BF), (0,) * 4, 2 * TOK * TOK * D, 4 << 20)(
        sel, tokens, router, parts
    )


def solution(mesh):
    split = Mesh(mesh.devices.reshape(-1, 2, G, G), ("z", "core", "x", "y"))
    every = ("z", "core", "x", "y")
    across = P(None, ("x", "y"))
    placed = (P(every, None), P(("z", "core")), P(), P(), across, across, across, P(("x", "y"), None))
    return jax.shard_map(on_device, mesh=split, in_specs=placed, out_specs=P(every, None), check_vma=False)
```

time: 123 us -> 99.3 us (0.81)
  waiting for transfers between devices: 47 us -> 29.4 us
  between operations: 13.5 us -> 0.15 us
  blocking collectives: 28.6 us -> 36.4 us
  starting transfers between devices: 8.3 us -> 15.3 us
  local copies, waits for them, and re-layouts: 10.4 us -> 6.9 us
  Pallas kernels: 12.4 us -> 9.48 us
    all_to_all x2 -> x3, waiting for transfers between devices: 43.7 us -> 27.3 us  [the longest x1 14.8 us: on_device(): rows = lax.all_to_all(send, 'y', 0, 0, tiled=True)]
    all_to_all x2, blocking collectives: 28.6 us -> 36.4 us  [the longest x1 19.3 us: on_device(): own = lax.all_to_all(send, 'x', 0, 0, tiled=True)]
    ppermute x0 -> x2, starting transfers between devices: none -> 3.83 us  [swap(): return lax.ppermute(half, 'core', [(0, 1), (1, 0)])]
    unnamed x28 -> x22, local copies, waits for them, and re-layouts: 10.4 us -> 6.9 us
    all_to_all x2 -> x3, starting transfers between devices: 8.26 us -> 11.5 us  [the longest x1 4.59 us: on_device(): rows = lax.all_to_all(send, 'y', 0, 0, tiled=True)]
    pallas_call x5 -> x6, Pallas kernels: 12.4 us -> 9.48 us  [the longest x1 3.49 us: on_device(): call(project_kernel, 'project', (shape((G, CHUNK, HS), BF), shape((G, 128...]
    all_gather x1 -> x0, waiting for transfers between devices: 2.65 us -> none  [on_device(): w_slice = lax.all_gather(piece, ('z', 'core'), axis=0, tiled=True)]
    ppermute x0 -> x2, waiting for transfers between devices: none -> 2.18 us  [swap(): return lax.ppermute(half, 'core', [(0, 1), (1, 0)])]
  transfers between devices with their start and end apart: 3 -> 5, of which waited for: 3 -> 4; matrix products, arithmetic and copies ran while one was open for 1% -> 1% of each run, Pallas kernels for 1% -> 1%
where the time goes in v4:
time: 99.3 us; the launch traced here: 98.6 us
  blocking collectives  36.4 us (37%)
  waiting for transfers between devices  29.4 us (30%)
  starting transfers between devices  15.3 us (15%)
  Pallas kernels  9.48 us (10%)
  local copies, waits for them, and re-layouts  6.9 us (7%)
    all_to_all x1, blocking collectives, on_device(): own = lax.all_to_all(send, 'x', 0, 0, tiled=True)  19.3 us
    all_to_all x1, blocking collectives, on_device(): parts = lax.all_to_all(send, ('x', 'y'), 0, 0, tiled=True)  17.1 us
    all_to_all x1, waiting for transfers between devices, on_device(): rows = lax.all_to_all(send, 'y', 0, 0, tiled=True)  14.8 us
    all_to_all x1, waiting for transfers between devices, on_device(): heads = lax.all_to_all(send, 'y', 0, 0, tiled=True)  7.33 us
    unnamed x22, local copies, waits for them, and re-layouts  6.9 us
    all_to_all x1, waiting for transfers between devices, on_device(): parts = lax.all_to_all(send, 'x', 0, 0, tiled=True)  5.07 us
    all_to_all x1, starting transfers between devices, on_device(): rows = lax.all_to_all(send, 'y', 0, 0, tiled=True)  4.59 us
    ppermute x2, starting transfers between devices, swap(): return lax.ppermute(half, 'core', [(0, 1), (1, 0)])  3.83 us
  transfers between devices with their start and end apart: 5, of which 4 were waited for; matrix products, arithmetic and copies ran while one was open for 1% of the time, Pallas kernels for 1%

profile of v4, /device:TPU:480, one launch (start us, length us, event | category | flops | bytes accessed | tf_op | source)
XLA Modules:
  0.0 98.6 jit_solution(5411965932965951047)
XLA Ops:
  0.0 1.2 %copy-done.1 = bf16[128,4096]{1,0:T(8,128)(2,1)S(1)} copy-done((bf16[128,4096]{1,0:T(8,128)(2,1)S(1)}, bf16[128,4096]{1,0:T(8,128)(2,1)}, u32[]{:S(2)}) %copy-start.1) | copy-done | bytes 1048600
  1.2 1.2 %copy-done.4 = bf16[4096,128]{1,0:T(8,128)(2,1)S(1)} copy-done((bf16[4096,128]{1,0:T(8,128)(2,1)S(1)}, bf16[4096,128]{1,0:T(8,128)(2,1)}, u32[]{:S(2)}) %copy-start.4) | copy-done | bytes 1048600
  2.5 0.9 copy-done.5
  3.4 0.9 copy-done.6
  4.4 0.7 copy-done.7
  5.0 0.7 copy-done.9
  5.7 1.2 %pack.1 = bf16[4,256,512]{2,1,0:T(8,128)(2,1)S(1)} custom-call(s32[1,256]{1,0:T(1,128)S(1)} %bitcast.5, bf16[4096]{0:T(1024)(128)(2,1)S(1)} %copy-done.9, bf16[128,4096]{1,0:T(8,128)(2,1)S(1)} %copy-done.1, bf16[4096,128]{1,0:T(8,128)(2,1)S(1)} %copy-done.4, bf16[32,4096]{1,0:T(8,128)(2,1)S(1)} %bitcast.3, bf16[32,4096]{1,0:T(8,128)(2,1)S(1)} %bitcast.4), custom_call_target="tpu_custom_call" | custom-call | flops 33554432 | bytes 2097152 | tf_op jit(solution)/shard_map/pack/pallas_call | solution.py:243
  6.9 0.0 copy-start.3
  7.0 19.3 %all_to_all.25.got_ref.own_ref = bf16[4,256,512]{2,1,0:T(8,128)(2,1)S(1)} all-to-all(bf16[4,256,512]{2,1,0:T(8,128)(2,1)S(1)} %pack.1), channel_id=1, replica_groups=mesh['z'=16,'core'=2,'x'=4,'y'=4] {'x'}, dimensions={0} | all-to-all | bytes 2097152 | tf_op jit(solution)/shard_map/all_to_all | solution.py:247
  26.3 0.0 copy-done.3
  26.3 0.2 spread.1
  26.5 1.2 %copy-done = bf16[4,384,512]{2,1,0:T(8,128)(2,1)} copy-done((bf16[4,384,512]{2,1,0:T(8,128)(2,1)}, bf16[4,384,512]{2,1,0:T(8,128)(2,1)S(1)}, u32[]{:S(2)}) %copy-start) | copy-done | bytes 1572888
  27.7 4.6 %all-to-all-start.1 = ((bf16[4,384,512]{2,1,0:T(8,128)(2,1)}), bf16[4,384,512]{2,1,0:T(8,128)(2,1)S(1)}, u32[]{:S(2)}, u32[]{:S(2)}) async-start(bf16[4,384,512]{2,1,0:T(8,128)(2,1)} %copy-done), calls=%async_computation.1 | async-start | bytes 3145728 | tf_op jit(solution)/shard_map/all_to_all | solution.py:252
  32.3 1.9 %collective-permute-start = (bf16[4,256,512]{2,1,0:T(8,128)(2,1)S(1)}, bf16[4,256,512]{2,1,0:T(8,128)(2,1)}, u32[]{:S(2)}, u32[]{:S(2)}) collective-permute-start(bf16[4,256,512]{2,1,0:T(8,128)(2,1)S(1)} %all_to_all.25.got_ref.own_ref), channel_id=1, source_target_pairs={{0,16},{16,0},{1,17},{17,1},{2,18},{18,2},{3,19},{19,3},{4,20},{20... | collective-permute-start | bytes 3145736 | tf_op jit(solution)/shard_map/ppermute | solution.py:241
  34.2 0.0 copy-done.8
  34.2 0.5 fusion
  34.8 2.2 %collective-permute-done.other_ref = bf16[4,256,512]{2,1,0:T(8,128)(2,1)} collective-permute-done((bf16[4,256,512]{2,1,0:T(8,128)(2,1)S(1)}, bf16[4,256,512]{2,1,0:T(8,128)(2,1)}, u32[]{:S(2)}, u32[]{:S(2)}) %collective-permute-start) | collective-permute-done | bytes 1048608 | tf_op jit(solution)/shard_map/ppermute | solution.py:241
  37.0 14.8 %all-to-all-done.1.rows_ref = bf16[4,384,512]{2,1,0:T(8,128)(2,1)S(1)} async-done(((bf16[4,384,512]{2,1,0:T(8,128)(2,1)}), bf16[4,384,512]{2,1,0:T(8,128)(2,1)S(1)}, u32[]{:S(2)}, u32[]{:S(2)}) %all-to-all-start.1) | async-done | bytes 1572896 | tf_op jit(solution)/shard_map/all_to_all | solution.py:252
  51.8 3.5 %project.1 = (bf16[4,384,128]{2,1,0:T(8,128)(2,1)}, bf16[4,128,512]{2,1,0:T(8,128)(2,1)S(1)}) custom-call(s32[1,256]{1,0:T(1,128)S(1)} %bitcast.6, bf16[4,384,512]{2,1,0:T(8,128)(2,1)S(1)} %all-to-all-done.1.rows_ref, bf16[4,256,512]{2,1,0:T(8,128)(2,1)S(1)} %all_to_all.25.got_ref.own_ref, bf16[4,256,512]{2,1,0:T(8,128)(2,1)} %collective-permute-done.other_ref), custom_call_target="tpu_custom_call" | custom-call | flops 671088640 | bytes 5242880 | tf_op jit(solution)/shard_map/project/pallas_call | solution.py:253
  55.3 3.5 %all-to-all-start.2 = ((bf16[4,384,128]{2,1,0:T(8,128)(2,1)}), bf16[4,384,128]{2,1,0:T(8,128)(2,1)S(1)}, u32[]{:S(2)}, u32[]{:S(2)}) async-start(bf16[4,384,128]{2,1,0:T(8,128)(2,1)} %get-tuple-element.7), calls=%async_computation.2 | async-start | bytes 786432 | tf_op jit(solution)/shard_map/all_to_all | solution.py:258
  58.8 1.9 %collective-permute-start.1 = (bf16[4,128,512]{2,1,0:T(8,128)(2,1)S(1)}, bf16[4,128,512]{2,1,0:T(8,128)(2,1)S(1)}, u32[]{:S(2)}, u32[]{:S(2)}) collective-permute-start(bf16[4,128,512]{2,1,0:T(8,128)(2,1)S(1)} %get-tuple-element.8.own_ref), channel_id=1, source_target_pairs={{0,16},{16,0},{1,17},{17,1},{2,18},{18,2},{3,19},{19,3},{4,20},{20... | collective-permute-start | bytes 1572872 | tf_op jit(solution)/shard_map/ppermute | solution.py:241
  60.7 0.3 fusion.1
  61.0 5.1 %all-to-all-done.2.parts_ref = bf16[4,384,128]{2,1,0:T(8,128)(2,1)S(1)} async-done(((bf16[4,384,128]{2,1,0:T(8,128)(2,1)}), bf16[4,384,128]{2,1,0:T(8,128)(2,1)S(1)}, u32[]{:S(2)}, u32[]{:S(2)}) %all-to-all-start.2) | async-done | bytes 393248 | tf_op jit(solution)/shard_map/all_to_all | solution.py:258
  66.1 0.9 turn.1
  67.0 3.5 %all-to-all-start.3 = ((bf16[4,384,128]{2,1,0:T(8,128)(2,1)}), bf16[4,384,128]{2,1,0:T(8,128)(2,1)S(1)}, u32[]{:S(2)}, u32[]{:S(2)}) async-start(bf16[4,384,128]{2,1,0:T(8,128)(2,1)} %turn.1), calls=%async_computation.3 | async-start | bytes 786432 | tf_op jit(solution)/shard_map/all_to_all | solution.py:262
  70.5 0.0 collective-permute-done.1.other_ref
  70.5 7.3 %all-to-all-done.3.heads_ref = bf16[4,384,128]{2,1,0:T(8,128)(2,1)S(1)} async-done(((bf16[4,384,128]{2,1,0:T(8,128)(2,1)}), bf16[4,384,128]{2,1,0:T(8,128)(2,1)S(1)}, u32[]{:S(2)}, u32[]{:S(2)}) %all-to-all-start.3) | async-done | bytes 393248 | tf_op jit(solution)/shard_map/all_to_all | solution.py:262
  77.8 1.7 %attend.1 = bf16[16,32,1024]{2,1,0:T(8,128)(2,1)S(1)} custom-call(s32[1,256]{1,0:T(1,128)S(1)} %bitcast.7, bf16[4,384,128]{2,1,0:T(8,128)(2,1)S(1)} %all-to-all-done.3.heads_ref, bf16[4,128,512]{2,1,0:T(8,128)(2,1)S(1)} %get-tuple-element.8.own_ref, bf16[4,128,512]{2,1,0:T(8,128)(2,1)S(1)} %collective-permute-done.1.other_ref), custom_call_target="tpu_custom_call" | custom-call | flops 681574400 | bytes 4194304 | tf_op jit(solution)/shard_map/attend/pallas_call | solution.py:263
  79.5 0.0 copy-start.2
  79.6 0.0 copy-start.10
  79.6 17.1 %all_to_all.26.parts_ref = bf16[16,32,1024]{2,1,0:T(8,128)(2,1)S(1)} all-to-all(bf16[16,32,1024]{2,1,0:T(8,128)(2,1)S(1)} %attend.1), channel_id=1, replica_groups=mesh['z'=16,'core'=2,'x'=4,'y'=4] {'x','y'}, dimensions={0} | all-to-all | bytes 2097152 | tf_op jit(solution)/shard_map/all_to_all | solution.py:267
  96.6 1.9 %finish.1 = bf16[128,4096]{1,0:T(8,128)(2,1)} custom-call(s32[1,256]{1,0:T(1,128)S(1)} %bitcast.8, bf16[128,4096]{1,0:T(8,128)(2,1)S(1)} %copy-done.2, bf16[4096]{0:T(1024)(128)(2,1)S(1)} %copy-done.10, bf16[16,32,1024]{2,1,0:T(8,128)(2,1)S(1)} %all_to_all.26.parts_ref), custom_call_target="tpu_custom_call" | custom-call | flops 134217728 | bytes 4194304 | tf_op jit(solution)/shard_map/finish/pallas_call | solution.py:268
  (13 shorter events, 0.1 us)
Async XLA Ops:
  0.0 1.2 %copy-start.1 = (bf16[128,4096]{1,0:T(8,128)(2,1)S(1)}, bf16[128,4096]{1,0:T(8,128)(2,1)}, u32[]{:S(2)}) copy-start(bf16[128,4096]{1,0:T(8,128)(2,1)} %tok_ref.1) | copy-start | bytes 3145732
  1.2 1.2 %copy-start.4 = (bf16[4096,128]{1,0:T(8,128)(2,1)S(1)}, bf16[4096,128]{1,0:T(8,128)(2,1)}, u32[]{:S(2)}) copy-start(bf16[4096,128]{1,0:T(8,128)(2,1)} %wq_hbm.1) | copy-start | bytes 3145732
  2.5 0.9 copy-start.5
  3.4 0.9 copy-start.6
  4.4 0.7 copy-start.7
  5.0 0.7 copy-start.9
  6.9 19.3 %copy-start.3 = (bf16[128,4096]{1,0:T(8,128)(2,1)S(1)}, bf16[128,4096]{1,0:T(8,128)(2,1)}, u32[]{:S(2)}) copy-start(bf16[128,4096]{1,0:T(8,128)(2,1)} %wout_hbm.1) | copy-start | bytes 3145732
  26.5 1.2 %copy-start = (bf16[4,384,512]{2,1,0:T(8,128)(2,1)}, bf16[4,384,512]{2,1,0:T(8,128)(2,1)S(1)}, u32[]{:S(2)}) copy-start(bf16[4,384,512]{2,1,0:T(8,128)(2,1)S(1)} %spread.1) | copy-start | bytes 4718596
  27.7 6.5 %copy-start.8 = (s32[256]{0:T(256)S(1)}, s32[256]{0:T(256)}, u32[]{:S(2)}) copy-start(s32[256]{0:T(256)} %param.9) | copy-start | bytes 3076
  27.7 24.1 %all-to-all-start.1 = ((bf16[4,384,512]{2,1,0:T(8,128)(2,1)}), bf16[4,384,512]{2,1,0:T(8,128)(2,1)S(1)}, u32[]{:S(2)}, u32[]{:S(2)}) async-start(bf16[4,384,512]{2,1,0:T(8,128)(2,1)} %copy-done), calls=%async_computation.1 | async-start | bytes 3145728 | tf_op jit(solution)/shard_map/all_to_all | solution.py:252
  32.3 4.7 %collective-permute-start = (bf16[4,256,512]{2,1,0:T(8,128)(2,1)S(1)}, bf16[4,256,512]{2,1,0:T(8,128)(2,1)}, u32[]{:S(2)}, u32[]{:S(2)}) collective-permute-start(bf16[4,256,512]{2,1,0:T(8,128)(2,1)S(1)} %all_to_all.25.got_ref.own_ref), channel_id=1, source_target_pairs={{0,16},{16,0},{1,17},{17,1},{2,18},{18,2},{3,19},{19,3},{4,20},{20... | collective-permute-start | bytes 3145736 | tf_op jit(solution)/shard_map/ppermute | solution.py:241
  55.3 10.8 %all-to-all-start.2 = ((bf16[4,384,128]{2,1,0:T(8,128)(2,1)}), bf16[4,384,128]{2,1,0:T(8,128)(2,1)S(1)}, u32[]{:S(2)}, u32[]{:S(2)}) async-start(bf16[4,384,128]{2,1,0:T(8,128)(2,1)} %get-tuple-element.7), calls=%async_computation.2 | async-start | bytes 786432 | tf_op jit(solution)/shard_map/all_to_all | solution.py:258
  58.8 11.7 %collective-permute-start.1 = (bf16[4,128,512]{2,1,0:T(8,128)(2,1)S(1)}, bf16[4,128,512]{2,1,0:T(8,128)(2,1)S(1)}, u32[]{:S(2)}, u32[]{:S(2)}) collective-permute-start(bf16[4,128,512]{2,1,0:T(8,128)(2,1)S(1)} %get-tuple-element.8.own_ref), channel_id=1, source_target_pairs={{0,16},{16,0},{1,17},{17,1},{2,18},{18,2},{3,19},{19,3},{4,20},{20... | collective-permute-start | bytes 1572872 | tf_op jit(solution)/shard_map/ppermute | solution.py:241
  67.0 10.8 %all-to-all-start.3 = ((bf16[4,384,128]{2,1,0:T(8,128)(2,1)}), bf16[4,384,128]{2,1,0:T(8,128)(2,1)S(1)}, u32[]{:S(2)}, u32[]{:S(2)}) async-start(bf16[4,384,128]{2,1,0:T(8,128)(2,1)} %turn.1), calls=%async_computation.3 | async-start | bytes 786432 | tf_op jit(solution)/shard_map/all_to_all | solution.py:262
  79.5 17.1 %copy-start.2 = (bf16[128,4096]{1,0:T(8,128)(2,1)S(1)}, bf16[128,4096]{1,0:T(8,128)(2,1)}, u32[]{:S(2)}) copy-start(bf16[128,4096]{1,0:T(8,128)(2,1)} %tok_ref.1) | copy-start | bytes 3145732
  79.6 17.1 %copy-start.10 = (bf16[4096]{0:T(1024)(128)(2,1)S(1)}, bf16[4096]{0:T(1024)(128)(2,1)}, u32[]{:S(2)}) copy-start(bf16[4096]{0:T(1024)(128)(2,1)} %router_ref.1) | copy-start | bytes 24580

commit v5 on v4

v5 whole, which is shorter than its diff:
```python
import jax
import jax.numpy as jnp
from jax import lax
from jax.experimental import pallas as pl
from jax.experimental.pallas import tpu as pltpu
from jax.sharding import Mesh
from jax.sharding import PartitionSpec as P

HS = 128
HQ = 16
KVH = 4
CAP = 32
N = 16
G = 4
TOK = 128
SEL = 256
D = 4096
Q = D // G
H = Q // 2
W = Q // 4
BF = jnp.bfloat16
F32 = jnp.float32
NT = (((1,), (1,)), ((), ()))
CHUNK = SEL + SEL // 2
VMEM = pltpu.VMEM


def one_hot(mask):
    return jnp.where(mask, 1.0, 0.0).astype(BF)


def iota(shape, axis):
    return lax.broadcasted_iota(jnp.int32, shape, axis)


def slots(sel, me):
    base = me * TOK
    first = jnp.sum(jnp.where(sel < base, 1.0, 0.0), axis=1, keepdims=True).astype(jnp.int32)
    mine = (sel >= base) & (sel < base + TOK)
    by_slot = one_hot((iota((CAP, SEL), 1) - first == iota((CAP, SEL), 0)) & mine)
    by_token = one_hot(iota((TOK, SEL), 0) + base == sel)
    return by_slot, by_token


def column(row):
    same = iota((SEL, SEL), 0) == iota((SEL, SEL), 1)
    return jnp.sum(jnp.where(same, row.astype(F32), 0.0), axis=1, keepdims=True).astype(jnp.int32)


def quarter():
    return 2 * lax.axis_index("core") + lax.axis_index("z") % 2


def pack_kernel(sel_hbm, gain_hbm, tok_hbm, wq_hbm, wk_hbm, wv_hbm, send_ref, sel_ref, gain_ref, tok_ref, sems):
    me, mine = lax.axis_index(("x", "y")), quarter()
    loads = []

    def load(source, target):
        loads.append(pltpu.make_async_copy(source, target, sems.at[len(loads)]))
        loads[-1].start()

    load(sel_hbm, sel_ref)
    for i in range(4):
        load(tok_hbm.at[pl.ds(i * 32, 32)], tok_ref.at[pl.ds(i * 32, 32)])
    load(gain_hbm, gain_ref)
    for t in range(G):
        start = pl.multiple_of(t * Q + mine * W, W)
        for i in range(4):
            load(wq_hbm.at[pl.ds(start + i * 64, 64)], send_ref.at[t, pl.ds(0, 64), pl.ds(i * 128, 128)])
        load(wk_hbm.at[:, pl.ds(start, W)], send_ref.at[t, pl.ds(64, 32), pl.ds(0, W)])
        load(wv_hbm.at[:, pl.ds(start, W)], send_ref.at[t, pl.ds(64, 32), pl.ds(W, W)])
    loads[0].wait()
    by_slot, by_token = slots(sel_ref[...], me)
    pick = lax.dot_general(by_slot, by_token, NT, preferred_element_type=F32).astype(BF)
    for copy in loads[1:6]:
        copy.wait()
    raw = jnp.dot(pick, tok_ref[...], preferred_element_type=F32)
    scale = lax.rsqrt(jnp.mean(raw * raw, axis=1, keepdims=True) + 1e-05)
    normed = (raw * scale * gain_ref[...].reshape(1, D).astype(F32)).astype(BF)
    for t in range(G):
        send_ref[t, 96:128, :] = normed[:, t * Q : t * Q + H]
        send_ref[t, 128:160, :] = normed[:, t * Q + H : (t + 1) * Q]
    for copy in loads[6:]:
        copy.wait()


def spread_kernel(got_ref, wout_hbm, send_ref, weight_ref, sems):
    core = lax.axis_index("core")
    loads = []
    for t in range(G):
        for i in range(2):
            loads.append(
                pltpu.make_async_copy(
                    wout_hbm.at[pl.ds(pl.multiple_of(core * 64, 64), 64), pl.ds(t * Q + i * H, H)],
                    send_ref.at[t, pl.ds(256 + i * 64, 64)],
                    sems.at[len(loads)],
                )
            )
            loads[-1].start()
    for s in range(G):
        rows = got_ref[s, 96:160, :]
        for t in range(G):
            send_ref[t, s * 64 : (s + 1) * 64, :] = rows
        weight_ref[s] = got_ref[s, :96, :]
    for copy in loads:
        copy.wait()


def project_kernel(sel_ref, rows_ref, w0_ref, w1_ref, w2_ref, w3_ref, send_ref, wout_ref, x_ref):
    mine = quarter()
    sel_row = sel_ref[...]
    owner = column(sel_row) >> 7
    first = jnp.sum(jnp.where(sel_row < owner * TOK, 1.0, 0.0), axis=1, keepdims=True).astype(jnp.int32)
    place = ((owner & 3) * G + (owner >> 2)) * CAP + iota((SEL, 1), 0) - first
    pick = one_hot(iota((SEL, N * CAP), 1) == place)
    for i in range(2):
        padded = jnp.concatenate(
            [rows_ref[s, t * 64 + i * 32 : t * 64 + (i + 1) * 32, :] for s in range(G) for t in range(G)], axis=0
        )
        dense = jnp.dot(pick, padded, preferred_element_type=F32).astype(BF)
        x_ref[2 * i], x_ref[2 * i + 1] = dense[:, :W], dense[:, W:]
    q = jnp.zeros((SEL, G * HS), F32)
    kv = jnp.zeros((SEL, G * 64), F32)
    for i, w_ref in enumerate((w0_ref, w1_ref, w2_ref, w3_ref)):
        x = x_ref[mine ^ i]
        w_q = jnp.concatenate(
            [
                jnp.concatenate([w_ref[s, :64, b * 128 : (b + 1) * 128] for b in range(4)], axis=0)
                for s in range(G)
            ],
            axis=1,
        )
        w_kv = jnp.concatenate([w_ref[s, 64:96, b * W : (b + 1) * W] for s in range(G) for b in range(2)], axis=0)
        q += jnp.dot(x, w_q, preferred_element_type=F32)
        kv += lax.dot_general(x, w_kv, NT, preferred_element_type=F32)
    to, frm = iota((SEL, SEL), 0), iota((SEL, SEL), 1)
    order = one_hot(frm == ((to >> 4) & 3) * 64 + ((to >> 3) & 1) * 32 + (to & 7) * 4 + (to >> 6))
    turned = lax.dot_general(order, kv.astype(BF), NT, preferred_element_type=F32).astype(BF)
    for t in range(G):
        send_ref[t, :SEL, :] = q[:, t * HS : (t + 1) * HS].astype(BF)
        send_ref[t, SEL : SEL + 64, :] = turned[t * 64 : (t + 1) * 64, :128]
        send_ref[t, SEL + 64 :, :] = turned[t * 64 : (t + 1) * 64, 128:]
        wout_ref[t] = rows_ref[t, 256:, :]


def turn_kernel(parts_ref, table_ref, send_ref):
    total = sum(parts_ref[s].astype(F32) for s in range(G))
    q = total[:SEL]
    mate = jnp.where(iota((SEL, HS), 1) % 2 == 0, pltpu.roll(q, HS - 1, 1), pltpu.roll(q, 1, 1))
    q = (q * table_ref[:SEL, :HS] + mate * table_ref[:SEL, HS:]).astype(BF)
    kv = jnp.concatenate([total[SEL : SEL + 64], total[SEL + 64 :]], axis=1)
    mate = jnp.where(iota((64, SEL), 0) % 2 == 0, pltpu.roll(kv, 63, 0), pltpu.roll(kv, 1, 0))
    kv = (kv * table_ref[SEL : SEL + 64] + mate * table_ref[SEL + 64 :]).astype(BF)
    for t in range(G):
        send_ref[t, :SEL, :] = q
        send_ref[t, SEL : SEL + 64, :] = kv[:, :128]
        send_ref[t, SEL + 64 :, :] = kv[:, 128:]


def attend_kernel(sel_ref, heads_ref, near_ref, far_ref, out_ref, mixed_ref, wout_ref):
    core = lax.axis_index("core")
    for i, w_ref in ((core, near_ref), (1 - core, far_ref)):
        for h in range(G):
            wout_ref[h, i] = jnp.concatenate([w_ref[h, :64, :], w_ref[h, 64:, :]], axis=1)
    halves = [
        heads_ref[:, SEL + i * 64 : SEL + (i + 1) * 64, :].astype(F32).reshape(G, G, 2, 8, 128) for i in range(2)
    ]
    keys, values = [
        jnp.concatenate(
            [
                jnp.concatenate([half[y, x, i] for x in range(G) for y in range(G)], axis=0).astype(BF)
                for half in halves
            ],
            axis=1,
        )
        for i in range(2)
    ]
    causal = iota((SEL, SEL), 0) >= iota((SEL, SEL), 1)
    for h in range(G):
        scores = jnp.dot(heads_ref[h, :SEL, :], keys, preferred_element_type=F32) * (HS**-0.5)
        scores = jnp.where(causal, scores, -1e30)
        weights = jnp.exp(scores - jnp.max(scores, axis=1, keepdims=True))
        probs = (weights / jnp.sum(weights, axis=1, keepdims=True)).astype(BF)
        mixed = lax.dot_general(probs, values, NT, preferred_element_type=F32)
        mixed_ref[:, h * HS : (h + 1) * HS] = mixed.astype(BF)
    sel_row = sel_ref[...]
    owner = sel_row >> 7
    first = jnp.sum(
        jnp.where(column(sel_row) < owner * TOK, 1.0, 0.0), axis=0, keepdims=True
    ).astype(jnp.int32)
    place = owner * CAP + iota((1, SEL), 1) - first
    put = one_hot(iota((N * CAP, SEL), 0) == place)
    update = jnp.dot(mixed_ref[...], wout_ref[...].reshape(G * HS, Q), preferred_element_type=F32).astype(BF)
    sent = jnp.dot(put, update, preferred_element_type=F32).astype(BF)
    out_ref[...] = sent.reshape(N, CAP, Q)


def gate_kernel(sel_ref, tok_ref, router_ref, gate_ref, put_ref):
    by_slot, by_token = slots(sel_ref[...], lax.axis_index(("x", "y")))
    put = lax.dot_general(by_token, by_slot, NT, preferred_element_type=F32).astype(BF)
    put_ref[...] = jnp.concatenate([put] * G, axis=1)
    router = router_ref[...].reshape(1, D).astype(F32)
    logit = jnp.sum(tok_ref[...].astype(F32) * router, axis=1, keepdims=True)
    gate_ref[...] = jnp.broadcast_to(1.0 / (1.0 + jnp.exp(-logit)), (TOK, 128))


def finish_kernel(tok_ref, gate_ref, put_ref, parts_ref, out_hbm, out_ref, sems):
    gate = gate_ref[:, :1]
    stores = []
    for y in range(G):
        terms = jnp.concatenate([parts_ref[x * G + y] for x in range(G)], axis=0)
        placed = jnp.dot(put_ref[...], terms, preferred_element_type=F32)
        part = slice(y * Q, (y + 1) * Q)
        out_ref[:, part] = (tok_ref[:, part].astype(F32) + gate * placed).astype(BF)
        there = pl.ds(y * Q, Q)
        stores.append(pltpu.make_async_copy(out_ref.at[:, there], out_hbm.at[:, there], sems.at[y]))
        stores[-1].start()
    for store in stores:
        store.wait()


def call(kernel, name, shapes, spaces, flops, moved, scratch=(), out=VMEM, vmem=40):
    where = {"v": VMEM, "h": pltpu.HBM, "a": pl.ANY}
    return pl.pallas_call(
        kernel,
        out_shape=shapes,
        in_specs=[pl.BlockSpec(memory_space=where[space]) for space in spaces],
        out_specs=jax.tree.map(lambda _: pl.BlockSpec(memory_space=out), shapes),
        scratch_shapes=scratch,
        compiler_params=pltpu.CompilerParams(vmem_limit_bytes=vmem * 1024 * 1024),
        cost_estimate=pl.CostEstimate(flops=flops, bytes_accessed=moved, transcendentals=0),
        name=name,
    )


def on_device(tokens, selected, norm_gain, router, w_query, w_key, w_value, w_out):
    y = lax.axis_index("y")
    shape = jax.ShapeDtypeStruct
    dma = pltpu.SemaphoreType.DMA
    sel = selected.reshape(1, SEL)
    def complete(piece, before=()):
        size = lax.axis_size("z")
        pairs = [(z, z ^ 1) for z in range(size)]
        near = lax.ppermute(piece, "z", pairs)
        cores = [(0, 1), (1, 0)]
        piece, before = lax.optimization_barrier((piece, before))
        return (piece, near, lax.ppermute(piece, "core", cores), lax.ppermute(near, "core", cores)), before

    send = call(
        pack_kernel, "pack", shape((G, 160, H), BF), "hhhhhh", 2 * CAP * TOK * D, 2 << 20,
        [VMEM((1, SEL), jnp.int32), VMEM((D,), BF), VMEM((TOK, D), BF), dma((6 + 6 * G,))], vmem=40,
    )(*[pltpu.with_memory_space_constraint(v, pltpu.HBM) for v in (sel, norm_gain, tokens, w_query, w_key.T, w_value.T)])
    got = lax.all_to_all(send, "x", 0, 0, tiled=True)
    send, piece = call(
        spread_kernel, "spread", (shape((G, 384, H), BF), shape((G, 96, H), BF)), "vh", 1 << 20, 3 << 20,
        [dma((2 * G,))],
    )(got, w_out)
    late, tokens_late, router, piece = lax.optimization_barrier((selected, tokens, router, piece))
    position = late.astype(F32)

    def turn(component, used):
        pair = (component // 2).astype(F32)
        inverse = jnp.exp(-(2.0 * pair / HS) * jnp.log(10000.0))
        return jnp.where(used, inverse, 0.0), jnp.where(component % 2 == 0, -1.0, 1.0)

    lane = jnp.arange(HS)
    inverse, sign = turn(lane, True)
    angle = position[:, None] * inverse[None, :]
    q_cos, q_sin = jnp.cos(angle), jnp.sin(angle) * sign[None, :]
    row = jnp.arange(64)
    inverse, sign = turn(8 * (G * (row // 16) + y) + row % 8, row % 16 < 8)
    angle = inverse[:, None] * position[None, :]
    k_cos, k_sin = jnp.cos(angle), jnp.sin(angle) * sign[:, None]
    table = jnp.concatenate([jnp.concatenate([q_cos, q_sin], axis=1), k_cos, k_sin], axis=0)
    gate, put = call(
        gate_kernel, "gate", (shape((TOK, 128), F32), shape((TOK, TOK), BF)), "vvv", TOK * D * 2, 2 << 20
    )(late.reshape(1, SEL), tokens_late, router)
    weights, (gate, put, table) = complete(piece, (gate, put, table))
    rows = lax.all_to_all(send, "y", 0, 0, tiled=True)
    rows, gate, put, table = lax.optimization_barrier((rows, gate, put, table))
    send, piece = call(
        project_kernel, "project", (shape((G, CHUNK, HS), BF), shape((G, 128, H), BF)), "vvvvvv",
        2 * SEL * Q * 1280, 5 << 20, [VMEM((4, SEL, W), BF)],
    )(sel, rows, *weights)
    w_near, w_far = piece, lax.ppermute(piece, "core", [(0, 1), (1, 0)])
    parts = lax.all_to_all(send, "x", 0, 0, tiled=True)
    send = call(turn_kernel, "turn", shape((G, CHUNK, HS), BF), "vv", SEL * HS * 20, 1 << 20)(parts, table)
    heads = lax.all_to_all(send, "y", 0, 0, tiled=True)
    send = call(
        attend_kernel, "attend", shape((N, CAP, Q), BF), "vvvv", 2 * SEL * 1024 * 1300, 4 << 20,
        [VMEM((SEL, G * HS), BF), VMEM((G, 2, 64, Q), BF)],
    )(sel, heads, w_near, w_far)
    parts = lax.all_to_all(send, ("x", "y"), 0, 0, tiled=True)
    return call(
        finish_kernel, "finish", shape((TOK, D), BF), "vvvv", 2 * TOK * TOK * D, 4 << 20,
        [VMEM((TOK, D), BF), dma((G,))], pltpu.HBM,
    )(tokens, gate, put, parts)


def solution(mesh):
    split = Mesh(mesh.devices.reshape(-1, 2, G, G), ("z", "core", "x", "y"))
    every = ("z", "core", "x", "y")
    across = P(None, ("x", "y"))
    placed = (P(every, None), P(("z", "core")), P(), P(), across, across, across, P(("x", "y"), None))
    return jax.shard_map(on_device, mesh=split, in_specs=placed, out_specs=P(every, None), check_vma=False)
```

time: 99.3 us -> 90.5 us (0.911)
  blocking collectives: 36.4 us -> 16.5 us
  starting transfers between devices: 15.3 us -> 24.6 us
  waiting for transfers between devices: 29.4 us -> 35 us
  local copies, waits for them, and re-layouts: 6.9 us -> 1.97 us
  Pallas kernels: 9.48 us -> 10.7 us
    all_to_all x1 -> x0, blocking collectives: 19.3 us -> none  [on_device(): own = lax.all_to_all(send, 'x', 0, 0, tiled=True)]
    all_to_all x0 -> x1, waiting for transfers between devices: none -> 10.9 us  [on_device(): got = lax.all_to_all(send, 'x', 0, 0, tiled=True)]
    all_to_all x1, waiting for transfers between devices: 14.8 us -> 6.16 us  [on_device(): rows = lax.all_to_all(send, 'y', 0, 0, tiled=True)]
    unnamed x22 -> x14, local copies, waits for them, and re-layouts: 6.9 us -> 1.97 us
    ppermute x2 -> x4, starting transfers between devices: 3.83 us -> 8.67 us  [the longest x1 2.92 us: complete(): near = lax.ppermute(piece, 'z', pairs)]
    all_to_all x0 -> x1, starting transfers between devices: none -> 4.31 us  [on_device(): got = lax.all_to_all(send, 'x', 0, 0, tiled=True)]
    ppermute x2 -> x4, waiting for transfers between devices: 2.18 us -> 5.21 us  [the longest x1 5.2 us: complete(): near = lax.ppermute(piece, 'z', pairs)]
    pallas_call x5 -> x6, Pallas kernels: 5.99 us -> 7.16 us  [the longest x1 2.85 us: on_device(): call(pack_kernel, 'pack', shape((G, 160, H), BF), 'hhhhhh', 2 * CAP * TOK...]
  transfers between devices with their start and end apart: 5 -> 8, of which waited for: 4 -> 5; matrix products, arithmetic and copies ran while one was open for 1% -> 1% of each run, Pallas kernels for 1% -> 1%
where the time goes in v5:
time: 90.5 us; the launch traced here: 90 us
  waiting for transfers between devices  35 us (39%)
  starting transfers between devices  24.6 us (27%)
  blocking collectives  16.5 us (18%)
  Pallas kernels  10.7 us (12%)
  local copies, waits for them, and re-layouts  1.97 us (2%)
  other arithmetic  0.91 us (1%)
    all_to_all x1, blocking collectives, on_device(): parts = lax.all_to_all(send, ('x', 'y'), 0, 0, tiled=True)  16.5 us
    all_to_all x1, waiting for transfers between devices, on_device(): got = lax.all_to_all(send, 'x', 0, 0, tiled=True)  10.9 us
    all_to_all x1, waiting for transfers between devices, on_device(): heads = lax.all_to_all(send, 'y', 0, 0, tiled=True)  7.33 us
    all_to_all x1, waiting for transfers between devices, on_device(): rows = lax.all_to_all(send, 'y', 0, 0, tiled=True)  6.16 us
    all_to_all x1, waiting for transfers between devices, on_device(): parts = lax.all_to_all(send, 'x', 0, 0, tiled=True)  5.42 us
    ppermute x1, waiting for transfers between devices, complete(): near = lax.ppermute(piece, 'z', pairs)  5.2 us
    all_to_all x1, starting transfers between devices, on_device(): rows = lax.all_to_all(send, 'y', 0, 0, tiled=True)  4.59 us
    all_to_all x1, starting transfers between devices, on_device(): got = lax.all_to_all(send, 'x', 0, 0, tiled=True)  4.31 us
  transfers between devices with their start and end apart: 8, of which 5 were waited for; matrix products, arithmetic and copies ran while one was open for 1% of the time, Pallas kernels for 1%

profile of v5, /device:TPU:480, one launch (start us, length us, event | category | flops | bytes accessed | tf_op | source)
XLA Modules:
  0.0 90.0 jit_solution(9303604568248140716)
XLA Ops:
  0.0 2.9 %pack.1 = bf16[4,160,512]{2,1,0:T(8,128)(2,1)} custom-call(s32[1,256]{1,0:T(1,128)} %bitcast.4, bf16[4096]{0:T(1024)(128)(2,1)} %gain_hbm.1, bf16[128,4096]{1,0:T(8,128)(2,1)} %tok_ref.2, bf16[4096,128]{1,0:T(8,128)(2,1)} %wq_hbm.1, bf16[32,4096]{1,0:T(8,128)(2,1)} %bitcast.8, bf16[32,4096]{1,0:T(8,128)(2,1)} %bitcast.9), custom_call_target="tpu_custom_call" | custom-call | flops 33554432 | bytes 2097152 | tf_op jit(solution)/shard_map/pack/pallas_call | solution.py:249
  2.9 4.3 %all-to-all-start = ((bf16[4,160,512]{2,1,0:T(8,128)(2,1)}), bf16[4,160,512]{2,1,0:T(8,128)(2,1)S(1)}, u32[]{:S(2)}, u32[]{:S(2)}) async-start(bf16[4,160,512]{2,1,0:T(8,128)(2,1)} %pack.1), calls=%async_computation | async-start | bytes 1310720 | tf_op jit(solution)/shard_map/all_to_all | solution.py:253
  7.2 10.9 %all-to-all-done.got_ref = bf16[4,160,512]{2,1,0:T(8,128)(2,1)S(1)} async-done(((bf16[4,160,512]{2,1,0:T(8,128)(2,1)}), bf16[4,160,512]{2,1,0:T(8,128)(2,1)S(1)}, u32[]{:S(2)}, u32[]{:S(2)}) %all-to-all-start) | async-done | bytes 655392 | tf_op jit(solution)/shard_map/all_to_all | solution.py:253
  18.1 0.0 copy-done.2
  18.1 0.3 spread.1
  18.3 0.0 copy-start.1
  18.3 1.2 %copy-done.1 = bf16[4,384,512]{2,1,0:T(8,128)(2,1)} copy-done((bf16[4,384,512]{2,1,0:T(8,128)(2,1)}, bf16[4,384,512]{2,1,0:T(8,128)(2,1)S(1)}, u32[]{:S(2)}) %copy-start.1) | copy-done | bytes 1572888
  19.5 4.6 %all-to-all-start.1 = ((bf16[4,384,512]{2,1,0:T(8,128)(2,1)}), bf16[4,384,512]{2,1,0:T(8,128)(2,1)S(1)}, u32[]{:S(2)}, u32[]{:S(2)}) async-start(bf16[4,384,512]{2,1,0:T(8,128)(2,1)} %copy-done.1), calls=%async_computation.1 | async-start | bytes 3145728 | tf_op jit(solution)/shard_map/all_to_all | solution.py:279
  24.1 0.0 copy-done.3
  24.2 2.9 %collective-permute-start = (bf16[4,96,512]{2,1,0:T(8,128)(2,1)S(1)}, bf16[4,96,512]{2,1,0:T(8,128)(2,1)}, u32[]{:S(2)}, u32[]{:S(2)}) collective-permute-start(bf16[4,96,512]{2,1,0:T(8,128)(2,1)S(1)} %get-tuple-element.37.w0_ref), channel_id=1, source_target_pairs={{0,32},{32,0},{64,96},{96,64},{128,160},{160,128},{192,224},{224,1... | collective-permute-start | bytes 1179656 | tf_op jit(solution)/shard_map/ppermute | solution.py:244
  27.1 0.3 multiply_cosine_fusion.1
  27.4 0.0 copy-done
  27.4 0.4 gate.1
  27.8 0.5 multiply_cosine_fusion
  28.4 1.9 %collective-permute-start.1 = (bf16[4,96,512]{2,1,0:T(8,128)(2,1)S(1)}, bf16[4,96,512]{2,1,0:T(8,128)(2,1)}, u32[]{:S(2)}, u32[]{:S(2)}) collective-permute-start(bf16[4,96,512]{2,1,0:T(8,128)(2,1)S(1)} %get-tuple-element.37.w0_ref), channel_id=1, source_target_pairs={{0,16},{16,0},{1,17},{17,1},{2,18},{18,2},{3,19},{19,3},{4,20},{20... | collective-permute-start | bytes 1179656 | tf_op jit(solution)/shard_map/ppermute | solution.py:247
  30.3 5.2 %collective-permute-done.w1_ref = bf16[4,96,512]{2,1,0:T(8,128)(2,1)} collective-permute-done((bf16[4,96,512]{2,1,0:T(8,128)(2,1)S(1)}, bf16[4,96,512]{2,1,0:T(8,128)(2,1)}, u32[]{:S(2)}, u32[]{:S(2)}) %collective-permute-start) | collective-permute-done | bytes 393248 | tf_op jit(solution)/shard_map/ppermute | solution.py:244
  35.5 1.9 %collective-permute-start.2 = (bf16[4,96,512]{2,1,0:T(8,128)(2,1)}, bf16[4,96,512]{2,1,0:T(8,128)(2,1)}, u32[]{:S(2)}, u32[]{:S(2)}) collective-permute-start(bf16[4,96,512]{2,1,0:T(8,128)(2,1)} %collective-permute-done.w1_ref), channel_id=1, source_target_pairs={{0,16},{16,0},{1,17},{17,1},{2,18},{18,2},{3,19},{19,3},{4,20},{20... | collective-permute-start | bytes 1179656 | tf_op jit(solution)/shard_map/ppermute | solution.py:247
  37.5 6.2 %all-to-all-done.1.rows_ref = bf16[4,384,512]{2,1,0:T(8,128)(2,1)S(1)} async-done(((bf16[4,384,512]{2,1,0:T(8,128)(2,1)}), bf16[4,384,512]{2,1,0:T(8,128)(2,1)S(1)}, u32[]{:S(2)}, u32[]{:S(2)}) %all-to-all-start.1) | async-done | bytes 1572896 | tf_op jit(solution)/shard_map/all_to_all | solution.py:279
  43.6 0.0 collective-permute-done.1.w2_ref
  43.6 0.0 collective-permute-done.2.w3_ref
  43.6 3.6 %project.1 = (bf16[4,384,128]{2,1,0:T(8,128)(2,1)}, bf16[4,128,512]{2,1,0:T(8,128)(2,1)S(1)}) custom-call(s32[1,256]{1,0:T(1,128)S(1)} %bitcast.6, bf16[4,384,512]{2,1,0:T(8,128)(2,1)S(1)} %all-to-all-done.1.rows_ref, bf16[4,96,512]{2,1,0:T(8,128)(2,1)S(1)} %get-tuple-element.37.w0_ref, bf16[4,96,512]{2,1,0:T(8,128)(2,1)} %collective-permute-done.w1_ref, ...), custom_call_target="tpu_custom_call" | custom-call | flops 671088640 | bytes 5242880 | tf_op jit(solution)/shard_map/project/pallas_call | solution.py:281
  47.2 0.8 copy-done.5
  48.0 3.6 %all-to-all-start.2 = ((bf16[4,384,128]{2,1,0:T(8,128)(2,1)}), bf16[4,384,128]{2,1,0:T(8,128)(2,1)S(1)}, u32[]{:S(2)}, u32[]{:S(2)}) async-start(bf16[4,384,128]{2,1,0:T(8,128)(2,1)} %get-tuple-element.38), calls=%async_computation.2 | async-start | bytes 786432 | tf_op jit(solution)/shard_map/all_to_all | solution.py:286
  51.6 1.9 %collective-permute-start.3 = (bf16[4,128,512]{2,1,0:T(8,128)(2,1)}, bf16[4,128,512]{2,1,0:T(8,128)(2,1)S(1)}, u32[]{:S(2)}, u32[]{:S(2)}) collective-permute-start(bf16[4,128,512]{2,1,0:T(8,128)(2,1)} %copy-done.5), channel_id=1, source_target_pairs={{0,16},{16,0},{1,17},{17,1},{2,18},{18,2},{3,19},{19,3},{4,20},{20... | collective-permute-start | bytes 1572872 | tf_op jit(solution)/shard_map/ppermute | solution.py:285
  53.5 5.4 %all-to-all-done.2.parts_ref = bf16[4,384,128]{2,1,0:T(8,128)(2,1)S(1)} async-done(((bf16[4,384,128]{2,1,0:T(8,128)(2,1)}), bf16[4,384,128]{2,1,0:T(8,128)(2,1)S(1)}, u32[]{:S(2)}, u32[]{:S(2)}) %all-to-all-start.2) | async-done | bytes 393248 | tf_op jit(solution)/shard_map/all_to_all | solution.py:286
  59.0 0.9 turn.1
  59.8 3.5 %all-to-all-start.3 = ((bf16[4,384,128]{2,1,0:T(8,128)(2,1)}), bf16[4,384,128]{2,1,0:T(8,128)(2,1)S(1)}, u32[]{:S(2)}, u32[]{:S(2)}) async-start(bf16[4,384,128]{2,1,0:T(8,128)(2,1)} %turn.1), calls=%async_computation.3 | async-start | bytes 786432 | tf_op jit(solution)/shard_map/all_to_all | solution.py:288
  63.3 0.0 collective-permute-done.3.far_ref
  63.3 7.3 %all-to-all-done.3.heads_ref = bf16[4,384,128]{2,1,0:T(8,128)(2,1)S(1)} async-done(((bf16[4,384,128]{2,1,0:T(8,128)(2,1)}), bf16[4,384,128]{2,1,0:T(8,128)(2,1)S(1)}, u32[]{:S(2)}, u32[]{:S(2)}) %all-to-all-start.3) | async-done | bytes 393248 | tf_op jit(solution)/shard_map/all_to_all | solution.py:288
  70.6 1.5 %attend.1 = bf16[16,32,1024]{2,1,0:T(8,128)(2,1)S(1)} custom-call(s32[1,256]{1,0:T(1,128)S(1)} %bitcast.7, bf16[4,384,128]{2,1,0:T(8,128)(2,1)S(1)} %all-to-all-done.3.heads_ref, bf16[4,128,512]{2,1,0:T(8,128)(2,1)S(1)} %copy-done.6, bf16[4,128,512]{2,1,0:T(8,128)(2,1)S(1)} %collective-permute-done.3.far_ref), custom_call_target="tpu_custom_call" | custom-call | flops 681574400 | bytes 4194304 | tf_op jit(solution)/shard_map/attend/pallas_call | solution.py:289
  72.2 16.5 %all_to_all.25.parts_ref = bf16[16,32,1024]{2,1,0:T(8,128)(2,1)S(1)} all-to-all(bf16[16,32,1024]{2,1,0:T(8,128)(2,1)S(1)} %attend.1), channel_id=1, replica_groups=mesh['z'=16,'core'=2,'x'=4,'y'=4] {'x','y'}, dimensions={0} | all-to-all | bytes 2097152 | tf_op jit(solution)/shard_map/all_to_all | solution.py:293
  88.7 1.2 %finish.1 = bf16[128,4096]{1,0:T(8,128)(2,1)} custom-call(bf16[128,4096]{1,0:T(8,128)(2,1)S(1)} %copy-done, f32[128,128]{1,0:T(8,128)S(1)} %get-tuple-element.34.gate_ref, bf16[128,128]{1,0:T(8,128)(2,1)S(1)} %get-tuple-element.35.put_ref, bf16[16,32,1024]{2,1,0:T(8,128)(2,1)S(1)} %all_to_all.25.parts_ref), custom_call_target="tpu_custom_call" | custom-call | flops 134217728 | bytes 4194304 | tf_op jit(solution)/shard_map/finish/pallas_call | solution.py:294
  (12 shorter events, 0.1 us)
Async XLA Ops:
  0.0 18.1 %copy-start.2 = (bf16[128,4096]{1,0:T(8,128)(2,1)S(1)}, bf16[128,4096]{1,0:T(8,128)(2,1)}, u32[]{:S(2)}) copy-start(bf16[128,4096]{1,0:T(8,128)(2,1)} %wout_hbm.1) | copy-start | bytes 3145732
  2.9 15.2 %all-to-all-start = ((bf16[4,160,512]{2,1,0:T(8,128)(2,1)}), bf16[4,160,512]{2,1,0:T(8,128)(2,1)S(1)}, u32[]{:S(2)}, u32[]{:S(2)}) async-start(bf16[4,160,512]{2,1,0:T(8,128)(2,1)} %pack.1), calls=%async_computation | async-start | bytes 1310720 | tf_op jit(solution)/shard_map/all_to_all | solution.py:253
  18.3 1.2 %copy-start.1 = (bf16[4,384,512]{2,1,0:T(8,128)(2,1)}, bf16[4,384,512]{2,1,0:T(8,128)(2,1)S(1)}, u32[]{:S(2)}) copy-start(bf16[4,384,512]{2,1,0:T(8,128)(2,1)S(1)} %get-tuple-element.23) | copy-start | bytes 4718596
  19.5 4.6 %copy-start.3 = (s32[256]{0:T(256)S(1)}, s32[256]{0:T(256)}, u32[]{:S(2)}) copy-start(s32[256]{0:T(256)} %param.9) | copy-start | bytes 3076
  19.5 7.9 %copy-start = (bf16[128,4096]{1,0:T(8,128)(2,1)S(1)}, bf16[128,4096]{1,0:T(8,128)(2,1)}, u32[]{:S(2)}) copy-start(bf16[128,4096]{1,0:T(8,128)(2,1)} %tok_ref.2) | copy-start | bytes 3145732
  19.5 7.9 %copy-start.4 = (bf16[4096]{0:T(1024)(128)(2,1)S(1)}, bf16[4096]{0:T(1024)(128)(2,1)}, u32[]{:S(2)}) copy-start(bf16[4096]{0:T(1024)(128)(2,1)} %router_ref) | copy-start | bytes 24580
  19.5 24.1 %all-to-all-start.1 = ((bf16[4,384,512]{2,1,0:T(8,128)(2,1)}), bf16[4,384,512]{2,1,0:T(8,128)(2,1)S(1)}, u32[]{:S(2)}, u32[]{:S(2)}) async-start(bf16[4,384,512]{2,1,0:T(8,128)(2,1)} %copy-done.1), calls=%async_computation.1 | async-start | bytes 3145728 | tf_op jit(solution)/shard_map/all_to_all | solution.py:279
  24.2 11.4 %collective-permute-start = (bf16[4,96,512]{2,1,0:T(8,128)(2,1)S(1)}, bf16[4,96,512]{2,1,0:T(8,128)(2,1)}, u32[]{:S(2)}, u32[]{:S(2)}) collective-permute-start(bf16[4,96,512]{2,1,0:T(8,128)(2,1)S(1)} %get-tuple-element.37.w0_ref), channel_id=1, source_target_pairs={{0,32},{32,0},{64,96},{96,64},{128,160},{160,128},{192,224},{224,1... | collective-permute-start | bytes 1179656 | tf_op jit(solution)/shard_map/ppermute | solution.py:244
  28.4 15.2 %collective-permute-start.1 = (bf16[4,96,512]{2,1,0:T(8,128)(2,1)S(1)}, bf16[4,96,512]{2,1,0:T(8,128)(2,1)}, u32[]{:S(2)}, u32[]{:S(2)}) collective-permute-start(bf16[4,96,512]{2,1,0:T(8,128)(2,1)S(1)} %get-tuple-element.37.w0_ref), channel_id=1, source_target_pairs={{0,16},{16,0},{1,17},{17,1},{2,18},{18,2},{3,19},{19,3},{4,20},{20... | collective-permute-start | bytes 1179656 | tf_op jit(solution)/shard_map/ppermute | solution.py:247
  35.5 8.1 %collective-permute-start.2 = (bf16[4,96,512]{2,1,0:T(8,128)(2,1)}, bf16[4,96,512]{2,1,0:T(8,128)(2,1)}, u32[]{:S(2)}, u32[]{:S(2)}) collective-permute-start(bf16[4,96,512]{2,1,0:T(8,128)(2,1)} %collective-permute-done.w1_ref), channel_id=1, source_target_pairs={{0,16},{16,0},{1,17},{17,1},{2,18},{18,2},{3,19},{19,3},{4,20},{20... | collective-permute-start | bytes 1179656 | tf_op jit(solution)/shard_map/ppermute | solution.py:247
  47.2 0.8 copy-start.5
  48.0 22.6 %copy-start.6 = (bf16[4,128,512]{2,1,0:T(8,128)(2,1)S(1)}, bf16[4,128,512]{2,1,0:T(8,128)(2,1)}, u32[]{:S(2)}) copy-start(bf16[4,128,512]{2,1,0:T(8,128)(2,1)} %copy-done.5) | copy-start | bytes 1572868
  48.0 10.9 %all-to-all-start.2 = ((bf16[4,384,128]{2,1,0:T(8,128)(2,1)}), bf16[4,384,128]{2,1,0:T(8,128)(2,1)S(1)}, u32[]{:S(2)}, u32[]{:S(2)}) async-start(bf16[4,384,128]{2,1,0:T(8,128)(2,1)} %get-tuple-element.38), calls=%async_computation.2 | async-start | bytes 786432 | tf_op jit(solution)/shard_map/all_to_all | solution.py:286
  51.6 11.7 %collective-permute-start.3 = (bf16[4,128,512]{2,1,0:T(8,128)(2,1)}, bf16[4,128,512]{2,1,0:T(8,128)(2,1)S(1)}, u32[]{:S(2)}, u32[]{:S(2)}) collective-permute-start(bf16[4,128,512]{2,1,0:T(8,128)(2,1)} %copy-done.5), channel_id=1, source_target_pairs={{0,16},{16,0},{1,17},{17,1},{2,18},{18,2},{3,19},{19,3},{4,20},{20... | collective-permute-start | bytes 1572872 | tf_op jit(solution)/shard_map/ppermute | solution.py:285
  59.8 10.8 %all-to-all-start.3 = ((bf16[4,384,128]{2,1,0:T(8,128)(2,1)}), bf16[4,384,128]{2,1,0:T(8,128)(2,1)S(1)}, u32[]{:S(2)}, u32[]{:S(2)}) async-start(bf16[4,384,128]{2,1,0:T(8,128)(2,1)} %turn.1), calls=%async_computation.3 | async-start | bytes 786432 | tf_op jit(solution)/shard_map/all_to_all | solution.py:288
